TPU v7x, 512 devices: a whole 4x4x16 slice. The times are simulated.
512 devices in a mesh: sfc: 128 (over y, z, core), blk: 4 (over x).
Axes of the slice: x: 4, y: 4, z: 16, core: 2. Of those that a mesh axis runs over, the one named last changes fastest.
Arguments:
- adjoint: float32 [5, 2048, 64, 128], P(None, 'sfc', 'blk'), may hold values from -6 to 6
- source: float32 [5, 2048, 64, 128], P(None, 'sfc', 'blk'), may hold values from -12 to 12
- velocity: bfloat16 [3, 2048, 64, 128], P(None, 'sfc', 'blk'), may hold values from -5 to 5
- dissip: bfloat16 [2048, 64, 128], P('sfc', 'blk'), may hold values from 0.5 to 2
- jacobian: float32 [3, 5, 5], replicated, may hold values from -2.5 to 2.5
- cut_counts: int32 [4096], P(('sfc', 'blk')), may hold values from 0 to 64, as said below
- cut_cell: int32 [262144], P(('sfc', 'blk')), may hold values from 0 to 4095
- face_angles: float32 [2, 262144], P(None, ('sfc', 'blk')), may hold values from -3.140625 to 3.140625
- face_area: float32 [262144], P(('sfc', 'blk')), may hold values from 0.2 to 1
- face_pressure: float32 [262144], P(('sfc', 'blk')), may hold values from 0.5 to 2
- tri_owner: int32 [262144, 1], P(('sfc', 'blk')), may hold values from 0 to 511; in each aligned block of 512 rows (0 to 511, 512 to 1023, ...) at most 2 rows name the same one
- tri_local: int32 [262144], P(('sfc', 'blk')), may hold values from 0 to 255
Outputs:
- relaxed: float32 [5, 2048, 64, 128], P(None, 'sfc', 'blk')
- sensitivity: float32 [3, 131072], P(None, ('sfc', 'blk'))
Inputs may be any that keep to these rules, and one draw needn't show every extreme that they name: `cut_counts`: each brick has at most 64 live cut faces; some brick has exactly 64, some have none. `tri_owner`: among the cut-face slots of one device (aligned blocks of 512 rows) no owner is named more than 2 times.
All inputs are finite; a program needn't handle non-finite values.
Results may differ from a plain program's by a relative error of at most 0.00065.
Values sent between devices are 32-bit elements; how exact they have to be, the bound alone decides.
No kernel may reach another device: no remote copies, remote signals or barrier semaphores. Data moves between devices by JAX's collectives and lax.ppermute only.
A program may use at most 192 MiB of HBM per device.

v0:
```python
import functools

import jax
import jax.numpy as jnp
from jax import lax
from jax.experimental import pallas as pl
from jax.experimental.pallas import tpu as pltpu
from jax.sharding import PartitionSpec as P

TRI_DEV = 256
OMEGA = 0.8
BIG = pltpu.CompilerParams(vmem_limit_bytes=40 * 1024 * 1024)


def dot_last(a, b):
    return lax.dot_general(a, b, (((1,), (1,)), ((), ())), preferred_element_type=jnp.float32)


def halves(x):
    high = x.astype(jnp.bfloat16)
    return high, (x - high.astype(jnp.float32)).astype(jnp.bfloat16)


def relax_factor(damping):
    return OMEGA / (6.0 * damping + 1.0)


def face_normals(angles):
    cosine = jnp.cos(angles)
    sine = jnp.sin(angles)
    across = cosine[1:2]
    return cosine[0:1] * across, sine[0:1] * across, sine[1:2]


def cell_rows(cell, rows):
    faces = cell.shape[1]
    at = lax.broadcasted_iota(jnp.int32, (rows, faces), 0)
    return jnp.where(at == cell // 16, 1.0, 0.0).astype(jnp.bfloat16)


def cell_depth(cell, per_brick):
    position = lax.broadcasted_iota(jnp.int32, cell.shape, 1)
    return position // per_brick * 16 + cell % 16


def face_weight(counts, area, per_brick):
    position = lax.broadcasted_iota(jnp.int32, area.shape, 1)
    brick = position // per_brick
    limit = jnp.zeros(area.shape, jnp.int32)
    for b in range(counts.shape[0]):
        limit = jnp.where(brick == b, counts[b], limit)
    return jnp.where(position % per_brick < limit, area, 0.0)


def turn(jac, direction, values):
    out = []
    for c in range(5):
        total = jac[direction, 0, c] * values[0]
        for k in range(1, 5):
            total = total + jac[direction, k, c] * values[k]
        out.append(total)
    return out


def coupled(jac, direction, side, speed, damping, values):
    factor = relax_factor(damping)
    scaled = (0.5 * side) * factor * speed
    spread = factor * damping
    turned = turn(jac, direction, values)
    return [scaled * turned[c] + spread * values[c] for c in range(5)]


def relax_row(jac, here, x_low, x_high, edge_low, edge_high, source, speed, damping, wall):
    rows, lanes = here[0].shape
    at_y = lax.broadcasted_iota(jnp.int32, (rows, lanes), 0)
    at_z = lax.broadcasted_iota(jnp.int32, (rows, lanes), 1)
    total = [None] * 5
    beside = [None] * 5
    for direction in range(3):
        jumps = []
        for c in range(5):
            if direction == 0:
                low, high = x_low[c], x_high[c]
            elif direction == 1:
                low = jnp.where(at_y == 0, edge_low[c], pltpu.roll(here[c], 1, 0))
                high = jnp.where(at_y == rows - 1, edge_high[c], pltpu.roll(here[c], rows - 1, 0))
            else:
                low = jnp.where(at_z == 0, 0.0, pltpu.roll(here[c], 1, 1))
                high = jnp.where(at_z == lanes - 1, 0.0, pltpu.roll(here[c], lanes - 1, 1))
            both = low + high
            beside[c] = both if beside[c] is None else beside[c] + both
            jumps.append(high - low)
        turned = turn(jac, direction, jumps)
        half = 0.5 * speed[direction]
        for c in range(5):
            part = half * turned[c]
            total[c] = part if total[c] is None else total[c] + part
    factor = relax_factor(damping)
    out = []
    for c in range(5):
        applied = total[c] + damping * (6.0 * here[c] - beside[c])
        if 1 <= c <= 3:
            for d in range(3):
                applied = applied + wall[c - 1][d] * here[1 + d]
        out.append(here[c] + factor * (source[c] - applied))
    return out


SYM = ((0, 1, 2), (1, 3, 4), (2, 4, 5))


def first_kernel(per_brick, jac, counts, cell_ref, angle_ref, area_ref, adjoint, source, velocity, dissip,
                 partial, walls, low_out, high_out):
    faces = cell_ref.shape[0]
    size_x, size_y, size_z = dissip.shape
    cell = cell_ref[...].reshape(1, faces)
    area = area_ref[...].reshape(1, faces)
    normal = face_normals(angle_ref[...])
    weight = face_weight(counts, area, per_brick)
    rows = cell_rows(cell, size_x * size_y)
    depth = cell_depth(cell, per_brick)
    at = lax.broadcasted_iota(jnp.int32, (size_z, faces), 0) == depth
    pairs = ((0, 0), (0, 1), (0, 2), (1, 1), (1, 2), (2, 2))
    for m, (a, b) in enumerate(pairs):
        value = weight * normal[a] * normal[b]
        high, low = halves(value)
        put_high = jnp.where(at, high.astype(jnp.float32), 0.0).astype(jnp.bfloat16)
        put_low = jnp.where(at, low.astype(jnp.float32), 0.0).astype(jnp.bfloat16)
        total = dot_last(rows, put_high) + dot_last(rows, put_low)
        walls[m] = total.reshape(size_x, size_y, size_z)

    def step(x, carry):
        here = [adjoint[c, x] for c in range(5)]
        below = jnp.maximum(x - 1, 0)
        above = jnp.minimum(x + 1, size_x - 1)
        has_low = jnp.where(x > 0, 1.0, 0.0)
        has_high = jnp.where(x < size_x - 1, 1.0, 0.0)
        x_low = [adjoint[c, below] * has_low for c in range(5)]
        x_high = [adjoint[c, above] * has_high for c in range(5)]
        zeros = [0.0] * 5
        src = [source[c, x] for c in range(5)]
        speed = [velocity[d, x].astype(jnp.float32) for d in range(3)]
        damping = dissip[x].astype(jnp.float32)
        sym = [walls[m, x] for m in range(6)]
        wall = [[sym[SYM[a][b]] for b in range(3)] for a in range(3)]
        out = relax_row(jac, here, x_low, x_high, zeros, zeros, src, speed, damping, wall)
        for c in range(5):
            partial[c, x] = out[c]
        fields = here + out + [speed[1], damping, speed[0]]
        for f, field in enumerate(fields):
            low_out[f, pl.ds(x, 1), :] = field[0:1]
            high_out[f, pl.ds(x, 1), :] = field[size_y - 1:size_y]
        return carry

    lax.fori_loop(0, size_x, step, 0)


def second_kernel(jac, from_low, from_high, *refs):
    sets, outs = (refs[0:4], refs[4:8]), refs[8:10]
    for (adjoint, partial, velocity, dissip), out, x in zip(sets, outs, (0, 15)):
        rows = adjoint.shape[2]
        speed_x = velocity[0, 0].astype(jnp.float32)
        speed_y = velocity[1, 0].astype(jnp.float32)
        damping = dissip[0].astype(jnp.float32)
        at_y = lax.broadcasted_iota(jnp.int32, speed_x.shape, 0)
        low = [from_low[c, x:x + 1, :] for c in range(5)]
        high = [from_high[c, x:x + 1, :] for c in range(5)]
        add_low = coupled(jac, 1, 1.0, speed_y[0:1], damping[0:1], low)
        add_high = coupled(jac, 1, -1.0, speed_y[rows - 1:rows], damping[rows - 1:rows], high)
        for c in range(5):
            out[c] = adjoint[c, 0]
            fixed = partial[c, 0]
            fixed = fixed + jnp.where(at_y == 0, add_low[c], 0.0)
            fixed = fixed + jnp.where(at_y == rows - 1, add_high[c], 0.0)
            out[5 + c] = fixed
        out[10] = speed_x
        out[11] = damping
        out[12] = jnp.concatenate(low + high + [jnp.zeros((rows - 10, speed_x.shape[1]), jnp.float32)], axis=0)


def third_kernel(per_brick, n_sfc, n_blk, jac, counts, cell_ref, angle_ref, area_ref, pressure_ref, owner_ref, local_ref,
                 partial, walls, source, velocity, dissip, y_own_low, y_own_high, y_low, y_high,
                 x_own_low, x_own_high, x_low, x_high, relaxed, message, field, edge_low, edge_high):
    faces = cell_ref.shape[0]
    size_x, size_y, size_z = dissip.shape
    for c in range(5):
        field[c, 1:1 + size_x] = partial[c]
    grab = lambda ref: [ref[c] for c in range(5)]
    add = coupled(jac, 0, 1.0, x_own_low[10], x_own_low[11], grab(x_low))
    for c in range(5):
        field[c, 1] = field[c, 1] + add[c]
    add = coupled(jac, 0, -1.0, x_own_high[10], x_own_high[11], grab(x_high))
    for c in range(5):
        field[c, size_x] = field[c, size_x] + add[c]
    add_low = coupled(jac, 1, 1.0, y_own_low[10], y_own_low[11], grab(y_low))
    add_high = coupled(jac, 1, -1.0, y_own_high[10], y_own_high[11], grab(y_high))
    for c in range(5):
        for x in range(size_x):
            field[c, 1 + x, 0:1, :] = field[c, 1 + x, 0:1, :] + add_low[c][x:x + 1]
            field[c, 1 + x, size_y - 1:size_y, :] = field[c, 1 + x, size_y - 1:size_y, :] + add_high[c][x:x + 1]
    add = coupled(jac, 0, -1.0, x_low[10], x_low[11], grab(x_own_low))
    for c in range(5):
        field[c, 0] = x_low[5 + c] + add[c]
    add = coupled(jac, 0, 1.0, x_high[10], x_high[11], grab(x_own_high))
    for c in range(5):
        field[c, size_x + 1] = x_high[5 + c] + add[c]
    at_x = lax.broadcasted_iota(jnp.int32, (size_x, size_z), 0)
    for edge, theirs, own, side, corner in ((edge_low, y_low, y_own_low, -1.0, 0), (edge_high, y_high, y_own_high, 1.0, 5)):
        add = coupled(jac, 1, side, theirs[10], theirs[11], grab(own))
        speed = theirs[12]
        damping = theirs[11]
        first = [x_low[12, corner + c:corner + c + 1, :] for c in range(5)]
        last = [x_high[12, corner + c:corner + c + 1, :] for c in range(5)]
        add_first = coupled(jac, 0, 1.0, speed[0:1], damping[0:1], first)
        add_last = coupled(jac, 0, -1.0, speed[size_x - 1:size_x], damping[size_x - 1:size_x], last)
        for c in range(5):
            value = theirs[5 + c] + add[c]
            value = value + jnp.where(at_x == 0, add_first[c], 0.0)
            edge[c] = value + jnp.where(at_x == size_x - 1, add_last[c], 0.0)

    def step(x, carry):
        here = [field[c, x + 1] for c in range(5)]
        below = [field[c, x] for c in range(5)]
        above = [field[c, x + 2] for c in range(5)]
        lows = [edge_low[c, pl.ds(x, 1), :] for c in range(5)]
        highs = [edge_high[c, pl.ds(x, 1), :] for c in range(5)]
        src = [source[c, x] for c in range(5)]
        speed = [velocity[d, x].astype(jnp.float32) for d in range(3)]
        damping = dissip[x].astype(jnp.float32)
        sym = [walls[m, x] for m in range(6)]
        wall = [[sym[SYM[a][b]] for b in range(3)] for a in range(3)]
        out = relax_row(jac, here, below, above, lows, highs, src, speed, damping, wall)
        for c in range(5):
            relaxed[c, x] = out[c]
        return carry

    lax.fori_loop(0, size_x, step, 0)

    cell = cell_ref[...].reshape(1, faces)
    area = area_ref[...].reshape(1, faces)
    normal = face_normals(angle_ref[...])
    weight = face_weight(counts, area, per_brick)
    rows = cell_rows(cell, size_x * size_y)
    depth = cell_depth(cell, per_brick)
    along = jnp.zeros((size_z, faces), jnp.float32)
    for c in range(3):
        turned = relaxed[1 + c].reshape(size_x * size_y, size_z).T
        high, low = halves(turned)
        picked = lax.dot_general(high, rows, (((1,), (0,)), ((), ())), preferred_element_type=jnp.float32)
        picked = picked + lax.dot_general(low, rows, (((1,), (0,)), ((), ())), preferred_element_type=jnp.float32)
        along = along + normal[c] * picked
    at = lax.broadcasted_iota(jnp.int32, (size_z, faces), 0) == depth
    project = jnp.sum(jnp.where(at, along, 0.0), axis=0, keepdims=True)
    scale = pressure_ref[...].reshape(1, faces) * weight * project
    owner = owner_ref[...].reshape(1, faces)
    label = local_ref[...].reshape(1, faces).astype(jnp.float32)
    block = min(faces, 128)
    number = owner.astype(jnp.float32)
    columns = [jnp.broadcast_to(number[:, t:t + block], (block, block)).T for t in range(0, faces, block)]
    before = (lax.broadcasted_iota(jnp.int32, (block, block), 0)
              < lax.broadcasted_iota(jnp.int32, (block, block), 1))
    ranks = []
    for u in range(faces // block):
        mine = number[:, u * block:(u + 1) * block]
        same = jnp.where((columns[u] == mine) & before, 1.0, 0.0)
        for t in range(u):
            same = same + jnp.where(columns[t] == mine, 1.0, 0.0)
        ranks.append(jnp.sum(same, axis=0, keepdims=True))
    rank = jnp.concatenate(ranks, axis=1)
    words = [normal[0] * scale, normal[1] * scale, normal[2] * scale, label]
    at_blk = owner % n_blk
    entries = []
    for b in range(n_blk):
        for j in range(2):
            keep = (at_blk == b) & (rank == float(j))
            entries += [jnp.where(keep, w, 0.0) for w in words]
    lanes = message.shape[1]
    entries.append(jnp.zeros((lanes - len(entries), faces), jnp.float32))
    high, low = halves(jnp.concatenate(entries, axis=0))
    target = lax.broadcasted_iota(jnp.int32, (n_sfc, faces), 0)
    target = jnp.where(target == owner // n_blk, 1.0, 0.0).astype(jnp.bfloat16)
    message[...] = dot_last(target, high) + dot_last(target, low)


def turn_kernel(words, got, out):
    out[...] = got[...].T[0:words]


def last_kernel(got, out):
    rows, lanes = got.shape
    tris = out.shape[1]
    at = lax.broadcasted_iota(jnp.int32, (tris, lanes), 0).astype(jnp.float32)
    total = jnp.zeros((16, tris), jnp.float32)
    for r in range(0, rows, 4):
        high, low = halves(got[r:r + 4, :])
        both = jnp.concatenate([high.astype(jnp.float32), jnp.zeros((4, lanes), jnp.float32), low.astype(jnp.float32), jnp.zeros((4, lanes), jnp.float32)], axis=0)
        hot = jnp.where(at == got[r + 3:r + 4, :], 1.0, 0.0).astype(jnp.bfloat16)
        total = total + dot_last(both.astype(jnp.bfloat16), hot)
    out[...] = total[0:3] + total[8:11]


def shift_both(axis, low, high):
    count = lax.axis_size(axis)
    forward = [(i, i + 1) for i in range(count - 1)]
    backward = [(j, i) for i, j in forward]
    return lax.ppermute(high, axis, forward), lax.ppermute(low, axis, backward)


def on_device(adjoint, source, velocity, dissip, jacobian, cut_counts, cut_cell, face_angles, face_area, face_pressure,
              tri_owner, tri_local):
    n_sfc, n_blk = lax.axis_size("sfc"), lax.axis_size("blk")
    _, size_x, size_y, size_z = adjoint.shape
    faces = cut_cell.shape[0]
    per_brick = faces // cut_counts.shape[0]
    f32 = jnp.float32
    smem = pl.BlockSpec(memory_space=pltpu.SMEM)
    vmem = pl.BlockSpec(memory_space=pltpu.VMEM)
    shape = jax.ShapeDtypeStruct
    owner = tri_owner.reshape(faces)

    strip = shape((13, 16, size_z), f32)
    partial, walls, y_low_out, y_high_out = pl.pallas_call(
        functools.partial(first_kernel, per_brick),
        in_specs=[smem, smem] + [vmem] * 7,
        out_specs=[vmem] * 4,
        out_shape=[shape(adjoint.shape, f32), shape((6, size_x, size_y, size_z), f32), strip, strip],
        compiler_params=BIG,
        name="first_step",
    )(jacobian, cut_counts, cut_cell, face_angles, face_area, adjoint, source, velocity, dissip)
    from_low, from_high = shift_both("blk", y_low_out, y_high_out)

    def rows_at(x):
        return [pl.BlockSpec((5, 1, size_y, size_z), lambda i: (0, x, 0, 0)),
                pl.BlockSpec((5, 1, size_y, size_z), lambda i: (0, x, 0, 0)),
                pl.BlockSpec((3, 1, size_y, size_z), lambda i: (0, x, 0, 0)),
                pl.BlockSpec((1, size_y, size_z), lambda i: (x, 0, 0))]

    whole = pl.BlockSpec((13, 16, size_z), lambda i: (0, 0, 0))
    x_low_out, x_high_out = pl.pallas_call(
        second_kernel,
        grid=(1,),
        in_specs=[smem, whole, whole] + rows_at(0) + rows_at(size_x - 1),
        out_specs=[whole, whole],
        out_shape=[strip, strip],
        name="edge_rows",
    )(jacobian, from_low, from_high, *([adjoint, partial, velocity, dissip] * 2))
    x_low, x_high = shift_both("sfc", x_low_out, x_high_out)

    relaxed, message = pl.pallas_call(
        functools.partial(third_kernel, per_brick, n_sfc, n_blk),
        in_specs=[smem, smem] + [vmem] * 19,
        out_specs=[vmem] * 2,
        out_shape=[shape(adjoint.shape, f32), shape((n_sfc, 128), f32)],
        scratch_shapes=[pltpu.VMEM((5, size_x + 2, size_y, size_z), f32),
                        pltpu.VMEM((5, size_x, size_z), f32), pltpu.VMEM((5, size_x, size_z), f32)],
        compiler_params=BIG,
        name="second_step",
    )(jacobian, cut_counts, cut_cell, face_angles, face_area, face_pressure, owner, tri_local,
      partial, walls, source, velocity, dissip, y_low_out, y_high_out, from_low, from_high,
      x_low_out, x_high_out, x_low, x_high)

    got = lax.all_to_all(message, "sfc", split_axis=0, concat_axis=0, tiled=True)
    words = 8 * n_blk
    turned = pl.pallas_call(
        functools.partial(turn_kernel, words),
        in_specs=[vmem],
        out_specs=vmem,
        out_shape=shape((words, n_sfc), f32),
        name="turn_words",
    )(got)
    got = lax.all_to_all(turned, "blk", split_axis=0, concat_axis=0, tiled=True)
    sensitivity = pl.pallas_call(
        last_kernel,
        in_specs=[vmem],
        out_specs=vmem,
        out_shape=shape((3, TRI_DEV), f32),
        name="sum_terms",
    )(got)
    return relaxed, sensitivity


def solution(mesh):
    return jax.shard_map(
        on_device,
        mesh=mesh,
        in_specs=(
            P(None, "sfc", "blk", None),
            P(None, "sfc", "blk", None),
            P(None, "sfc", "blk", None),
            P("sfc", "blk", None),
            P(),
            P(("sfc", "blk")),
            P(("sfc", "blk")),
            P(None, ("sfc", "blk")),
            P(("sfc", "blk")),
            P(("sfc", "blk")),
            P(("sfc", "blk"), None),
            P(("sfc", "blk")),
        ),
        out_specs=(P(None, "sfc", "blk", None), P(None, ("sfc", "blk"))),
        check_vma=False,
    )
```

profile of v0, /device:TPU:1, one launch (start us, length us, event | category | flops | bytes accessed | tf_op | source)
XLA Modules:
  0.0 85.7 jit_solution(13592070313790479235)
XLA Ops:
  0.7 0.7 copy.19.jac
  1.4 1.1 %copy-done = f32[5,16,16,128]{3,2,1,0:T(8,128)S(1)} copy-done((f32[5,16,16,128]{3,2,1,0:T(8,128)S(1)}, f32[5,16,16,128]{3,2,1,0:T(8,128)}, u32[]{:S(2)}) %copy-start) | copy-done | bytes 655384
  2.5 0.9 %copy-done.3 = bf16[3,16,16,128]{3,2,1,0:T(8,128)(2,1)S(1)} copy-done((bf16[3,16,16,128]{3,2,1,0:T(8,128)(2,1)S(1)}, bf16[3,16,16,128]{3,2,1,0:T(8,128)(2,1)}, u32[]{:S(2)}) %copy-start.3) | copy-done | bytes 196632
  3.4 1.1 %copy-done.5 = f32[5,16,16,128]{3,2,1,0:T(8,128)S(1)} copy-done((f32[5,16,16,128]{3,2,1,0:T(8,128)S(1)}, f32[5,16,16,128]{3,2,1,0:T(8,128)}, u32[]{:S(2)}) %copy-start.5) | copy-done | bytes 655384
  4.5 0.8 copy-done.7
  5.4 3.6 %first_step.1 = (f32[5,16,16,128]{3,2,1,0:T(8,128)S(1)}, f32[6,16,16,128]{3,2,1,0:T(8,128)S(1)}, f32[13,16,128]{2,1,0:T(8,128)S(1)}, f32[13,16,128]{2,1,0:T(8,128)S(1)}) custom-call(f32[3,5,5]{2,1,0:T(8,128)S(1)} %copy.19.jac, s32[8]{0:T(128)S(1)} %copy-done.23, s32[512]{0:T(512)S(1)} %copy-done.18, f32[2,512]{1,0:T(2,128)S(1)} %copy-done.17, ...), custom_call_target="tpu_custom_call" | custom-call | tf_op jit(solution)/shard_map/first_step/pallas_call | solution.py:322
  9.0 0.8 copy-done.1
  9.9 1.3 %collective-permute-start.1 = (f32[13,16,128]{2,1,0:T(8,128)S(1)}, f32[13,16,128]{2,1,0:T(8,128)S(1)}, u32[]{:S(2)}, u32[]{:S(2)}) collective-permute-start(f32[13,16,128]{2,1,0:T(8,128)S(1)} %get-tuple-element.12.y_own_low), channel_id=1, source_target_pairs={{1,0},{2,1},{3,2},{5,4},{6,5},{7,6},{9,8},{10,9},{11,10},{13,12},{... | collective-permute-start | bytes 319496 | tf_op jit(solution)/shard_map/ppermute | solution.py:306
  11.2 4.6 %collective-permute-start = (f32[13,16,128]{2,1,0:T(8,128)S(1)}, f32[13,16,128]{2,1,0:T(8,128)S(1)}, u32[]{:S(2)}, u32[]{:S(2)}) collective-permute-start(f32[13,16,128]{2,1,0:T(8,128)S(1)} %get-tuple-element.13.y_own_high), channel_id=1, source_target_pairs={{0,1},{1,2},{2,3},{4,5},{5,6},{6,7},{8,9},{9,10},{10,11},{12,13},{... | collective-permute-start | bytes 319496 | tf_op jit(solution)/shard_map/ppermute | solution.py:306
  15.9 1.5 %collective-permute-done.from_low.y_low = f32[13,16,128]{2,1,0:T(8,128)S(1)} collective-permute-done((f32[13,16,128]{2,1,0:T(8,128)S(1)}, f32[13,16,128]{2,1,0:T(8,128)S(1)}, u32[]{:S(2)}, u32[]{:S(2)}) %collective-permute-start) | collective-permute-done | bytes 106528 | tf_op jit(solution)/shard_map/ppermute | solution.py:306
  17.4 0.6 copy-done.11
  18.1 1.8 %edge_rows.1 = (f32[13,16,128]{2,1,0:T(8,128)}, f32[13,16,128]{2,1,0:T(8,128)}) custom-call(f32[3,5,5]{2,1,0:T(8,128)} %copy-done.13, f32[13,16,128]{2,1,0:T(8,128)} %copy-done.11, f32[13,16,128]{2,1,0:T(8,128)} %copy-done.9, f32[5,16,16,128]{3,2,1,0:T(8,128)} %refs_4_.1, f32[5,16,16,128]{3,2,1,0:T(8,128)} %copy-done.1, bf16[3,16,16,128]{3,2,1,0:T(8,128)(2,1)} %velocity.3, ...), custom_call_target="tpu_custom_call" | custom-call | tf_op jit(solution)/shard_map/edge_rows/pallas_call | solution.py:339
  19.9 9.5 %collective-permute-start.3 = (f32[13,16,128]{2,1,0:T(8,128)}, f32[13,16,128]{2,1,0:T(8,128)S(1)}, u32[]{:S(2)}, u32[]{:S(2)}) collective-permute-start(f32[13,16,128]{2,1,0:T(8,128)} %get-tuple-element.14.x_own_low), channel_id=1, source_target_pairs={{4,0},{8,4},{12,8},{16,12},{20,16},{24,20},{28,24},{32,28},{36,32}... | collective-permute-start | bytes 319496 | tf_op jit(solution)/shard_map/ppermute | solution.py:306
  29.4 1.9 %collective-permute-start.2 = (f32[13,16,128]{2,1,0:T(8,128)}, f32[13,16,128]{2,1,0:T(8,128)S(1)}, u32[]{:S(2)}, u32[]{:S(2)}) collective-permute-start(f32[13,16,128]{2,1,0:T(8,128)} %get-tuple-element.15.x_own_high), channel_id=1, source_target_pairs={{0,4},{4,8},{8,12},{12,16},{16,20},{20,24},{24,28},{28,32},{32,36}... | collective-permute-start | bytes 319496 | tf_op jit(solution)/shard_map/ppermute | solution.py:306
  31.3 2.0 %collective-permute-done.2.x_low = f32[13,16,128]{2,1,0:T(8,128)S(1)} collective-permute-done((f32[13,16,128]{2,1,0:T(8,128)}, f32[13,16,128]{2,1,0:T(8,128)S(1)}, u32[]{:S(2)}, u32[]{:S(2)}) %collective-permute-start.2) | collective-permute-done | bytes 106528 | tf_op jit(solution)/shard_map/ppermute | solution.py:306
  33.4 0.9 %copy-done.10 = f32[13,16,128]{2,1,0:T(8,128)S(1)} copy-done((f32[13,16,128]{2,1,0:T(8,128)S(1)}, f32[13,16,128]{2,1,0:T(8,128)}, u32[]{:S(2)}) %copy-start.10) | copy-done | bytes 106520
  34.3 0.9 %copy-done.12 = f32[13,16,128]{2,1,0:T(8,128)S(1)} copy-done((f32[13,16,128]{2,1,0:T(8,128)S(1)}, f32[13,16,128]{2,1,0:T(8,128)}, u32[]{:S(2)}) %copy-start.12) | copy-done | bytes 106520
  35.2 0.9 %copy-done.15 = f32[13,16,128]{2,1,0:T(8,128)S(1)} copy-done((f32[13,16,128]{2,1,0:T(8,128)S(1)}, f32[13,16,128]{2,1,0:T(8,128)}, u32[]{:S(2)}) %copy-start.15) | copy-done | bytes 106520
  36.1 0.9 %copy-done.16 = f32[13,16,128]{2,1,0:T(8,128)S(1)} copy-done((f32[13,16,128]{2,1,0:T(8,128)S(1)}, f32[13,16,128]{2,1,0:T(8,128)}, u32[]{:S(2)}) %copy-start.16) | copy-done | bytes 106520
  37.0 4.2 %second_step.1 = (f32[5,16,16,128]{3,2,1,0:T(8,128)}, f32[128,128]{1,0:T(8,128)S(1)}) custom-call(f32[3,5,5]{2,1,0:T(8,128)S(1)} %copy-done.14, s32[8]{0:T(128)S(1)} %copy-done.23, s32[512]{0:T(512)S(1)} %copy-done.18, f32[2,512]{1,0:T(2,128)S(1)} %copy-done.17, f32[512]{0:T(512)S(1)} %copy-done.19, f32[512]{0:T(512)S(1)} %copy-done.20, s32[512]{0:T(512)S(1)} %bitcast.8, ...), custom_call_target="tpu_custom_call" | custom-call | tf_op jit(solution)/shard_map/second_step/pallas_call | solution.py:349
  41.2 32.2 %all_to_all.22 = f32[128,1,128]{2,1,0:T(1,128)} all-to-all(f32[128,1,128]{2,1,0:T(1,128)S(1)} %bitcast.7), channel_id=1, replica_groups=mesh['sfc'=128,'blk'=4] {'sfc'}, dimensions={0} | all-to-all | bytes 131072 | tf_op jit(solution)/shard_map/all_to_all | solution.py:362
  73.3 1.5 %turn_words.1 = f32[32,128]{1,0:T(8,128)} custom-call(f32[128,128]{1,0:T(8,128)} %bitcast.9), custom_call_target="tpu_custom_call" | custom-call | tf_op jit(solution)/shard_map/turn_words/pallas_call | solution.py:364
  74.9 9.3 %all_to_all.23 = f32[4,8,128]{2,1,0:T(8,128)} all-to-all(f32[4,8,128]{2,1,0:T(8,128)} %bitcast.10), channel_id=1, replica_groups=mesh['sfc'=128,'blk'=4] {'blk'}, dimensions={0} | all-to-all | bytes 32768 | tf_op jit(solution)/shard_map/all_to_all | solution.py:371
  84.1 1.6 %sum_terms.1 = f32[3,256]{1,0:T(4,128)} custom-call(f32[32,128]{1,0:T(8,128)} %bitcast.11), custom_call_target="tpu_custom_call" | custom-call | tf_op jit(solution)/shard_map/sum_terms/pallas_call | solution.py:372
  (40 shorter events, 0.2 us)
Async XLA Ops:
  0.6 0.8 copy-start.19
  1.4 1.1 %copy-start = (f32[5,16,16,128]{3,2,1,0:T(8,128)S(1)}, f32[5,16,16,128]{3,2,1,0:T(8,128)}, u32[]{:S(2)}) copy-start(f32[5,16,16,128]{3,2,1,0:T(8,128)} %refs_4_.1) | copy-start | bytes 1966084
  2.5 0.9 %copy-start.3 = (bf16[3,16,16,128]{3,2,1,0:T(8,128)(2,1)S(1)}, bf16[3,16,16,128]{3,2,1,0:T(8,128)(2,1)}, u32[]{:S(2)}) copy-start(bf16[3,16,16,128]{3,2,1,0:T(8,128)(2,1)} %velocity.3) | copy-start | bytes 589828
  3.4 1.1 %copy-start.5 = (f32[5,16,16,128]{3,2,1,0:T(8,128)S(1)}, f32[5,16,16,128]{3,2,1,0:T(8,128)}, u32[]{:S(2)}) copy-start(f32[5,16,16,128]{3,2,1,0:T(8,128)} %source.3) | copy-start | bytes 1966084
  4.5 0.8 copy-start.7
  5.4 3.7 %copy-start.13 = (f32[3,5,5]{2,1,0:T(8,128)}, f32[3,5,5]{2,1,0:T(8,128)S(1)}, u32[]{:S(2)}) copy-start(f32[3,5,5]{2,1,0:T(8,128)S(1)} %copy.19.jac) | copy-start | bytes 904
  9.0 0.8 copy-start.1
  9.9 6.0 %collective-permute-start.1 = (f32[13,16,128]{2,1,0:T(8,128)S(1)}, f32[13,16,128]{2,1,0:T(8,128)S(1)}, u32[]{:S(2)}, u32[]{:S(2)}) collective-permute-start(f32[13,16,128]{2,1,0:T(8,128)S(1)} %get-tuple-element.12.y_own_low), channel_id=1, source_target_pairs={{1,0},{2,1},{3,2},{5,4},{6,5},{7,6},{9,8},{10,9},{11,10},{13,12},{... | collective-permute-start | bytes 319496 | tf_op jit(solution)/shard_map/ppermute | solution.py:306
  11.2 6.3 %collective-permute-start = (f32[13,16,128]{2,1,0:T(8,128)S(1)}, f32[13,16,128]{2,1,0:T(8,128)S(1)}, u32[]{:S(2)}, u32[]{:S(2)}) collective-permute-start(f32[13,16,128]{2,1,0:T(8,128)S(1)} %get-tuple-element.13.y_own_high), channel_id=1, source_target_pairs={{0,1},{1,2},{2,3},{4,5},{5,6},{6,7},{8,9},{9,10},{10,11},{12,13},{... | collective-permute-start | bytes 319496 | tf_op jit(solution)/shard_map/ppermute | solution.py:306
  15.9 1.5 %copy-start.9 = (f32[13,16,128]{2,1,0:T(8,128)}, f32[13,16,128]{2,1,0:T(8,128)S(1)}, u32[]{:S(2)}) copy-start(f32[13,16,128]{2,1,0:T(8,128)S(1)} %collective-permute-done.1.from_high.y_high) | copy-start | bytes 319492
  18.1 15.3 %copy-start.2 = (f32[5,16,16,128]{3,2,1,0:T(8,128)S(1)}, f32[5,16,16,128]{3,2,1,0:T(8,128)}, u32[]{:S(2)}) copy-start(f32[5,16,16,128]{3,2,1,0:T(8,128)} %copy-done.1) | copy-start | bytes 1966084
  18.1 15.3 %copy-start.4 = (bf16[3,16,16,128]{3,2,1,0:T(8,128)(2,1)S(1)}, bf16[3,16,16,128]{3,2,1,0:T(8,128)(2,1)}, u32[]{:S(2)}) copy-start(bf16[3,16,16,128]{3,2,1,0:T(8,128)(2,1)} %velocity.3) | copy-start | bytes 589828
  18.1 15.3 %copy-start.6 = (f32[5,16,16,128]{3,2,1,0:T(8,128)S(1)}, f32[5,16,16,128]{3,2,1,0:T(8,128)}, u32[]{:S(2)}) copy-start(f32[5,16,16,128]{3,2,1,0:T(8,128)} %source.3) | copy-start | bytes 1966084
  18.1 15.3 %copy-start.8 = (bf16[16,16,128]{2,1,0:T(8,128)(2,1)S(1)}, bf16[16,16,128]{2,1,0:T(8,128)(2,1)}, u32[]{:S(2)}) copy-start(bf16[16,16,128]{2,1,0:T(8,128)(2,1)} %dissip.3) | copy-start | bytes 196612
  18.1 15.3 %copy-start.14 = (f32[3,5,5]{2,1,0:T(8,128)S(1)}, f32[3,5,5]{2,1,0:T(8,128)}, u32[]{:S(2)}) copy-start(f32[3,5,5]{2,1,0:T(8,128)} %copy-done.13) | copy-start | bytes 904
  19.9 13.5 %copy-start.22 = (s32[512]{0:T(512)S(1)}, s32[512]{0:T(512)}, u32[]{:S(2)}) copy-start(s32[512]{0:T(512)} %local_ref.1) | copy-start | bytes 6148
  19.9 11.4 %collective-permute-start.3 = (f32[13,16,128]{2,1,0:T(8,128)}, f32[13,16,128]{2,1,0:T(8,128)S(1)}, u32[]{:S(2)}, u32[]{:S(2)}) collective-permute-start(f32[13,16,128]{2,1,0:T(8,128)} %get-tuple-element.14.x_own_low), channel_id=1, source_target_pairs={{4,0},{8,4},{12,8},{16,12},{20,16},{24,20},{28,24},{32,28},{36,32}... | collective-permute-start | bytes 319496 | tf_op jit(solution)/shard_map/ppermute | solution.py:306
  29.4 4.0 %copy-start.21 = (s32[512,1]{0,1:T(1,128)S(1)}, s32[512,1]{0,1:T(1,128)}, u32[]{:S(2)}) copy-start(s32[512,1]{0,1:T(1,128)} %param.22) | copy-start | bytes 6148
  29.4 4.0 %copy-start.20 = (f32[512]{0:T(512)S(1)}, f32[512]{0:T(512)}, u32[]{:S(2)}) copy-start(f32[512]{0:T(512)} %pressure_ref.1) | copy-start | bytes 6148
  29.4 3.9 %collective-permute-start.2 = (f32[13,16,128]{2,1,0:T(8,128)}, f32[13,16,128]{2,1,0:T(8,128)S(1)}, u32[]{:S(2)}, u32[]{:S(2)}) collective-permute-start(f32[13,16,128]{2,1,0:T(8,128)} %get-tuple-element.15.x_own_high), channel_id=1, source_target_pairs={{0,4},{4,8},{8,12},{12,16},{16,20},{20,24},{24,28},{28,32},{32,36}... | collective-permute-start | bytes 319496 | tf_op jit(solution)/shard_map/ppermute | solution.py:306
  33.4 0.9 %copy-start.10 = (f32[13,16,128]{2,1,0:T(8,128)S(1)}, f32[13,16,128]{2,1,0:T(8,128)}, u32[]{:S(2)}) copy-start(f32[13,16,128]{2,1,0:T(8,128)} %copy-done.9) | copy-start | bytes 319492
  34.3 0.9 %copy-start.12 = (f32[13,16,128]{2,1,0:T(8,128)S(1)}, f32[13,16,128]{2,1,0:T(8,128)}, u32[]{:S(2)}) copy-start(f32[13,16,128]{2,1,0:T(8,128)} %copy-done.11) | copy-start | bytes 319492
  35.2 0.9 %copy-start.15 = (f32[13,16,128]{2,1,0:T(8,128)S(1)}, f32[13,16,128]{2,1,0:T(8,128)}, u32[]{:S(2)}) copy-start(f32[13,16,128]{2,1,0:T(8,128)} %get-tuple-element.14.x_own_low) | copy-start | bytes 319492
  36.1 0.9 %copy-start.16 = (f32[13,16,128]{2,1,0:T(8,128)S(1)}, f32[13,16,128]{2,1,0:T(8,128)}, u32[]{:S(2)}) copy-start(f32[13,16,128]{2,1,0:T(8,128)} %get-tuple-element.15.x_own_high) | copy-start | bytes 319492
  (4 other events, 2.9 us)
where the time goes:
time: 86.7 us; the launch traced here: 85.7 us
  blocking collectives  41.5 us (48%)
  starting transfers between devices  17.2 us (20%)
  Pallas kernels  12.7 us (15%)
  local copies, waits for them, and re-layouts  9.77 us (11%)
  waiting for transfers between devices  3.69 us (4%)
    all_to_all x1, blocking collectives, on_device(): lax.all_to_all(message, 'sfc', split_axis=0, concat_axis=0, tiled=True)  32.2 us
    ppermute x2, starting transfers between devices, shift_both(): lax.ppermute(low, axis, backward)  10.7 us
    unnamed x49, local copies, waits for them, and re-layouts  9.77 us
    all_to_all x1, blocking collectives, on_device(): got = lax.all_to_all(turned, 'blk', split_axis=0, concat_axis=0, tiled=True)  9.28 us
    ppermute x2, starting transfers between devices, shift_both(): lax.ppermute(high, axis, forward)  6.5 us
    pallas_call x1, Pallas kernels, on_device(): pl.pallas_call(functools.partial(third_kernel, per_brick, n_sfc, n_blk),...  4.2 us
    pallas_call x1, Pallas kernels, on_device(): pl.pallas_call(functools.partial(first_kernel, per_brick), in_specs=[smem...  3.64 us
    ppermute x2, waiting for transfers between devices, shift_both(): lax.ppermute(high, axis, forward)  3.54 us
  transfers between devices with their start and end apart: 4, of which 3 were waited for; matrix products, arithmetic and copies ran while one was open for 0% of the time, Pallas kernels for 0%

commit v1 on v0

v1 whole, which is shorter than its diff:
```python
import functools

import jax
import jax.numpy as jnp
from jax import lax
from jax.experimental import pallas as pl
from jax.experimental.pallas import tpu as pltpu
from jax.sharding import PartitionSpec as P

TRI_DEV = 256
OMEGA = 0.8
ROOM = pltpu.CompilerParams(vmem_limit_bytes=20 * 1024 * 1024)

SMALL = pltpu.CompilerParams(vmem_limit_bytes=4 * 1024 * 1024)


def dot_last(a, b):
    return lax.dot_general(a, b, (((1,), (1,)), ((), ())), preferred_element_type=jnp.float32)


def halves(x):
    high = x.astype(jnp.bfloat16)
    return high, (x - high.astype(jnp.float32)).astype(jnp.bfloat16)


def relax_factor(damping):
    return OMEGA / (6.0 * damping + 1.0)


def face_normals(angles):
    cosine = jnp.cos(angles)
    sine = jnp.sin(angles)
    across = cosine[1:2]
    return cosine[0:1] * across, sine[0:1] * across, sine[1:2]


def cell_rows(cell, rows):
    faces = cell.shape[1]
    at = lax.broadcasted_iota(jnp.int32, (rows, faces), 0)
    return jnp.where(at == cell // 16, 1.0, 0.0).astype(jnp.bfloat16)


def cell_depth(cell, per_brick):
    position = lax.broadcasted_iota(jnp.int32, cell.shape, 1)
    return position // per_brick * 16 + cell % 16


def face_weight(counts, area, per_brick):
    position = lax.broadcasted_iota(jnp.int32, area.shape, 1)
    brick = position // per_brick
    limit = jnp.zeros(area.shape, jnp.int32)
    for b in range(counts.shape[0]):
        limit = jnp.where(brick == b, counts[b], limit)
    return jnp.where(position % per_brick < limit, area, 0.0)


def turn(jac, direction, values):
    out = []
    for c in range(5):
        total = jac[0, direction, c] * values[0]
        for k in range(1, 5):
            total = total + jac[k, direction, c] * values[k]
        out.append(total)
    return out


def coupled(jac, direction, side, speed, damping, values):
    factor = relax_factor(damping)
    scaled = (0.5 * side) * factor * speed
    spread = factor * damping
    turned = turn(jac, direction, values)
    return [scaled * turned[c] + spread * values[c] for c in range(5)]


def relax_row(jac, here, x_low, x_high, edge_low, edge_high, source, speed, damping, wall):
    rows, lanes = here[0].shape
    at_y = lax.broadcasted_iota(jnp.int32, (rows, lanes), 0)
    at_z = lax.broadcasted_iota(jnp.int32, (rows, lanes), 1)
    total = [None] * 5
    beside = [None] * 5
    for direction in range(3):
        jumps = []
        for c in range(5):
            if direction == 0:
                low, high = x_low[c], x_high[c]
            elif direction == 1:
                low = jnp.where(at_y == 0, edge_low[c], pltpu.roll(here[c], 1, 0))
                high = jnp.where(at_y == rows - 1, edge_high[c], pltpu.roll(here[c], rows - 1, 0))
            else:
                low = jnp.where(at_z == 0, 0.0, pltpu.roll(here[c], 1, 1))
                high = jnp.where(at_z == lanes - 1, 0.0, pltpu.roll(here[c], lanes - 1, 1))
            both = low + high
            beside[c] = both if beside[c] is None else beside[c] + both
            jumps.append(high - low)
        turned = turn(jac, direction, jumps)
        half = 0.5 * speed[direction]
        for c in range(5):
            part = half * turned[c]
            total[c] = part if total[c] is None else total[c] + part
    factor = relax_factor(damping)
    out = []
    for c in range(5):
        applied = total[c] + damping * (6.0 * here[c] - beside[c])
        if 1 <= c <= 3:
            for d in range(3):
                applied = applied + wall[c - 1][d] * here[1 + d]
        out.append(here[c] + factor * (source[c] - applied))
    return out


SYM = ((0, 1, 2), (1, 3, 4), (2, 4, 5))


def start_all(pairs, sems):
    copies = [pltpu.make_async_copy(src, dst, sems.at[i]) for i, (src, dst) in enumerate(pairs)]
    for copy in copies:
        copy.start()
    return copies


def wait_all(copies):
    for copy in copies:
        copy.wait()


def first_kernel(per_brick, jac, counts, cell_hbm, angle_hbm, area_hbm, adjoint_hbm, source_hbm, velocity_hbm, dissip_hbm,
                 partial, walls, near_out, far_out, first_out, last_out,
                 cell_ref, angle_ref, area_ref, field, source, velocity, dissip, edges, sems):
    size_x, size_y, size_z = dissip.shape
    copies = start_all([(cell_hbm, cell_ref), (angle_hbm, angle_ref), (area_hbm, area_ref),
                        (adjoint_hbm, field.at[:, pl.ds(1, size_x)]), (velocity_hbm, velocity),
                        (dissip_hbm, dissip), (source_hbm, source)], sems)
    side = 1 - lax.axis_index("blk") % 2
    faces = cell_ref.shape[0]
    blank = jnp.zeros((size_y, size_z), jnp.float32)
    for c in range(5):
        field[c, 0] = blank
        field[c, size_x + 1] = blank
    wait_all(copies[:3])
    cell = cell_ref[...].reshape(1, faces)
    area = area_ref[...].reshape(1, faces)
    normal = face_normals(angle_ref[...])
    weight = face_weight(counts, area, per_brick)
    rows = cell_rows(cell, size_x * size_y)
    depth = cell_depth(cell, per_brick)
    at = lax.broadcasted_iota(jnp.int32, (size_z, faces), 0) == depth
    hot = jnp.where(at, 1.0, 0.0).astype(jnp.bfloat16)
    rows = jnp.concatenate([rows, rows], axis=1)
    pairs = ((0, 0), (0, 1), (0, 2), (1, 1), (1, 2), (2, 2))
    for m in range(0, 6, 2):
        put = []
        for a, b in pairs[m:m + 2]:
            high, low = halves(weight * normal[a] * normal[b])
            put.append(jnp.concatenate([hot * high, hot * low], axis=1))
        total = dot_last(rows, jnp.concatenate(put, axis=0))
        walls[m] = total[:, :size_z].reshape(size_x, size_y, size_z)
        walls[m + 1] = total[:, size_z:].reshape(size_x, size_y, size_z)
    wait_all(copies[3:])

    def step(x, carry):
        here = [field[c, x + 1] for c in range(5)]
        below = [field[c, x] for c in range(5)]
        above = [field[c, x + 2] for c in range(5)]
        zeros = [0.0] * 5
        src = [source[c, x] for c in range(5)]
        speed = [velocity[d, x].astype(jnp.float32) for d in range(3)]
        damping = dissip[x].astype(jnp.float32)
        sym = [walls[m, x] for m in range(6)]
        wall = [[sym[SYM[a][b]] for b in range(3)] for a in range(3)]
        out = relax_row(jac, here, below, above, zeros, zeros, src, speed, damping, wall)
        for c in range(5):
            partial[c, x] = out[c]
        fields = here + out + [speed[1], damping, speed[0]]
        for f, edge in enumerate(fields):
            edges[side, f, pl.ds(x, 1), :] = edge[0:1]
            edges[1 - side, f, pl.ds(x, 1), :] = edge[size_y - 1:size_y]
        return carry

    lax.fori_loop(0, size_x, step, 0, unroll=2)
    near_out[...] = edges[0]
    far_out[...] = edges[1]
    for out, x in ((first_out, 0), (last_out, size_x - 1)):
        for c in range(5):
            out[c] = field[c, x + 1]
            out[5 + c] = partial[c, x]
        out[10] = velocity[0, x].astype(jnp.float32)
        out[11] = dissip[x].astype(jnp.float32)
        out[12] = velocity[1, x].astype(jnp.float32)


def second_kernel(jac, from_near, from_far, first, last, near_out, far_out, both):
    rows, lanes = first.shape[1:]
    at_y = lax.broadcasted_iota(jnp.int32, (rows, lanes), 0)
    odd = lax.axis_index("blk") % 2 == 1
    side = 1 - lax.axis_index("core")
    for mine, place, x in ((first, side, 0), (last, 1 - side, from_near.shape[1] - 1)):
        speed_y = mine[12]
        damping = mine[11]
        near = [from_near[c, x:x + 1, :] for c in range(5)]
        far = [from_far[c, x:x + 1, :] for c in range(5)]
        low = [jnp.where(odd, a, b) for a, b in zip(near, far)]
        high = [jnp.where(odd, b, a) for a, b in zip(near, far)]
        add_low = coupled(jac, 1, 1.0, speed_y[0:1], damping[0:1], low)
        add_high = coupled(jac, 1, -1.0, speed_y[rows - 1:rows], damping[rows - 1:rows], high)
        for c in range(5):
            both[place, c] = mine[c]
            fixed = mine[5 + c]
            fixed = fixed + jnp.where(at_y == 0, add_low[c], 0.0)
            both[place, 5 + c] = fixed + jnp.where(at_y == rows - 1, add_high[c], 0.0)
        both[place, 10] = mine[10]
        both[place, 11] = damping
        both[place, 12] = jnp.concatenate(low + high + [jnp.zeros((rows - 10, lanes), jnp.float32)], axis=0)
    near_out[...] = both[0]
    far_out[...] = both[1]


def third_kernel(per_brick, parts, jac, counts, cell_ref, angle_ref, area_ref, pressure_ref, owner_hbm, local_ref,
                 partial, walls, source_hbm, velocity_hbm, dissip_hbm, y_own_near, y_own_far, y_near, y_far,
                 x_own_near, x_own_far, x_near, x_far, relaxed_hbm, message,
                 field, edge_low, edge_high, relaxed, source, velocity, dissip, owner_ref, sems, out_sem):
    copies = start_all([(velocity_hbm, velocity), (dissip_hbm, dissip), (source_hbm, source), (owner_hbm, owner_ref)], sems)
    faces = cell_ref.shape[0]
    size_x, size_y, size_z = dissip.shape
    for c in range(5):
        field[c, 1:1 + size_x] = partial[c]
    odd_y = lax.axis_index("blk") % 2 == 1
    odd_x = lax.axis_index("core") == 1

    class Sorted:
        def __init__(self, odd, when_odd, when_even):
            self.odd, self.when_odd, self.when_even = odd, when_odd, when_even

        def __getitem__(self, at):
            return jnp.where(self.odd, self.when_odd[at], self.when_even[at])

    y_low, y_high = Sorted(odd_y, y_near, y_far), Sorted(odd_y, y_far, y_near)
    y_own_low, y_own_high = Sorted(odd_y, y_own_near, y_own_far), Sorted(odd_y, y_own_far, y_own_near)
    x_low, x_high = Sorted(odd_x, x_near, x_far), Sorted(odd_x, x_far, x_near)
    x_own_low, x_own_high = Sorted(odd_x, x_own_near, x_own_far), Sorted(odd_x, x_own_far, x_own_near)
    grab = lambda ref: [ref[c] for c in range(5)]
    add = coupled(jac, 0, 1.0, x_own_low[10], x_own_low[11], grab(x_low))
    for c in range(5):
        field[c, 1] = field[c, 1] + add[c]
    add = coupled(jac, 0, -1.0, x_own_high[10], x_own_high[11], grab(x_high))
    for c in range(5):
        field[c, size_x] = field[c, size_x] + add[c]
    add_low = coupled(jac, 1, 1.0, y_own_low[10], y_own_low[11], grab(y_low))
    add_high = coupled(jac, 1, -1.0, y_own_high[10], y_own_high[11], grab(y_high))
    for c in range(5):
        for x in range(size_x):
            field[c, 1 + x, 0:1, :] = field[c, 1 + x, 0:1, :] + add_low[c][x:x + 1]
            field[c, 1 + x, size_y - 1:size_y, :] = field[c, 1 + x, size_y - 1:size_y, :] + add_high[c][x:x + 1]
    add = coupled(jac, 0, -1.0, x_low[10], x_low[11], grab(x_own_low))
    for c in range(5):
        field[c, 0] = x_low[5 + c] + add[c]
    add = coupled(jac, 0, 1.0, x_high[10], x_high[11], grab(x_own_high))
    for c in range(5):
        field[c, size_x + 1] = x_high[5 + c] + add[c]
    at_x = lax.broadcasted_iota(jnp.int32, (size_x, size_z), 0)
    for edge, theirs, own, side, corner in ((edge_low, y_low, y_own_low, -1.0, 0), (edge_high, y_high, y_own_high, 1.0, 5)):
        add = coupled(jac, 1, side, theirs[10], theirs[11], grab(own))
        speed = theirs[12]
        damping = theirs[11]
        first = [x_low[12, corner + c:corner + c + 1, :] for c in range(5)]
        last = [x_high[12, corner + c:corner + c + 1, :] for c in range(5)]
        add_first = coupled(jac, 0, 1.0, speed[0:1], damping[0:1], first)
        add_last = coupled(jac, 0, -1.0, speed[size_x - 1:size_x], damping[size_x - 1:size_x], last)
        for c in range(5):
            value = theirs[5 + c] + add[c]
            value = value + jnp.where(at_x == 0, add_first[c], 0.0)
            edge[c] = value + jnp.where(at_x == size_x - 1, add_last[c], 0.0)

    def step(x, carry):
        here = [field[c, x + 1] for c in range(5)]
        below = [field[c, x] for c in range(5)]
        above = [field[c, x + 2] for c in range(5)]
        lows = [edge_low[c, pl.ds(x, 1), :] for c in range(5)]
        highs = [edge_high[c, pl.ds(x, 1), :] for c in range(5)]
        src = [source[c, x] for c in range(5)]
        speed = [velocity[d, x].astype(jnp.float32) for d in range(3)]
        damping = dissip[x].astype(jnp.float32)
        sym = [walls[m, x] for m in range(6)]
        wall = [[sym[SYM[a][b]] for b in range(3)] for a in range(3)]
        out = relax_row(jac, here, below, above, lows, highs, src, speed, damping, wall)
        for c in range(5):
            relaxed[c, x] = out[c]
        return carry

    wait_all(copies)
    lax.fori_loop(0, size_x, step, 0, unroll=2)
    done = pltpu.make_async_copy(relaxed, relaxed_hbm, out_sem)
    done.start()

    cell = cell_ref[...].reshape(1, faces)
    area = area_ref[...].reshape(1, faces)
    normal = face_normals(angle_ref[...])
    weight = face_weight(counts, area, per_brick)
    rows = cell_rows(cell, size_x * size_y)
    depth = cell_depth(cell, per_brick)
    turned = []
    for c in range(3):
        high, low = halves(relaxed[1 + c].reshape(size_x * size_y, size_z).T)
        turned.append(jnp.concatenate([high, low], axis=1))
    picked = jnp.dot(jnp.concatenate(turned, axis=0), jnp.concatenate([rows, rows], axis=0),
                     preferred_element_type=jnp.float32)
    along = normal[0] * picked[:size_z] + normal[1] * picked[size_z:2 * size_z] + normal[2] * picked[2 * size_z:]
    at = lax.broadcasted_iota(jnp.int32, (size_z, faces), 0) == depth
    project = jnp.sum(jnp.where(at, along, 0.0), axis=0, keepdims=True)
    scale = pressure_ref[...].reshape(1, faces) * weight * project
    owner = owner_ref[...].reshape(1, faces)
    label = local_ref[...].reshape(1, faces).astype(jnp.float32)
    block = min(faces, 128)
    number = owner.astype(jnp.float32)
    columns = [jnp.broadcast_to(number[:, t:t + block], (block, block)).T for t in range(0, faces, block)]
    before = (lax.broadcasted_iota(jnp.int32, (block, block), 0)
              < lax.broadcasted_iota(jnp.int32, (block, block), 1))
    ranks = []
    for u in range(faces // block):
        mine = number[:, u * block:(u + 1) * block]
        same = jnp.where((columns[u] == mine) & before, 1.0, 0.0)
        for t in range(u):
            same = same + jnp.where(columns[t] == mine, 1.0, 0.0)
        ranks.append(jnp.sum(same, axis=0, keepdims=True))
    rank = jnp.concatenate(ranks, axis=1)
    n_y, n_z, n_c, n_x = parts
    words = [normal[0] * scale, normal[1] * scale, normal[2] * scale, label]
    pair = [jnp.where(rank == float(j), w, 0.0) for j in range(2) for w in words]
    high, low = halves(jnp.concatenate(pair * n_z, axis=0))
    at_x, at_c, at_z, at_y = owner % n_x, owner // n_x % n_c, owner // (n_x * n_c) % n_z, owner // (n_x * n_c * n_z)
    lane = lax.broadcasted_iota(jnp.int32, (8 * n_z, faces), 0)
    hot = jnp.where(lane // 8 == at_z, 1.0, 0.0).astype(jnp.bfloat16)
    target = lax.broadcasted_iota(jnp.int32, (n_y * n_c * n_x, faces), 0)
    target = jnp.where(target == (at_y * n_c + at_c) * n_x + at_x, 1.0, 0.0).astype(jnp.bfloat16)
    message[...] = dot_last(jnp.concatenate([target, target], axis=1),
                            jnp.concatenate([hot * high, hot * low], axis=1))
    done.wait()


def turn_kernel(got, out):
    turned = got[...].T
    blank = jnp.zeros((turned.shape[0], out.shape[1] - turned.shape[1]), jnp.float32)
    out[...] = jnp.concatenate([turned, blank], axis=1)


def last_kernel(used, got, out):
    tris = out.shape[1]
    rows = got.shape[0]
    fold = max(1, min(128 // used, rows // 8))
    rows = rows // fold
    packed = jnp.concatenate([got[g * rows:(g + 1) * rows, 0:used] for g in range(fold)], axis=1)
    at = lax.broadcasted_iota(jnp.int32, (tris, fold * used), 0).astype(jnp.float32)
    values, hot = [], []
    for r in range(0, rows, 8):
        tile = packed[r:r + 8]
        for j in range(2):
            high, low = halves(tile if j == 0 else pltpu.roll(tile, 4, 0))
            both = jnp.concatenate([high.astype(jnp.float32), low.astype(jnp.float32)], axis=0)
            values.append(both.astype(jnp.bfloat16))
            hot.append(jnp.where(at == tile[4 * j + 3:4 * j + 4], 1.0, 0.0).astype(jnp.bfloat16))
    total = dot_last(jnp.concatenate(values, axis=1), jnp.concatenate(hot, axis=1))
    out[...] = total[0:3] + total[8:11]


def swap(axis, near, far):
    count = lax.axis_size(axis)
    inside = [(i, i ^ 1) for i in range(count)]
    across = [(i, i + 1 if i % 2 else i - 1) for i in range(1, count - 1)]
    from_far = lax.ppermute(far, axis, across)
    return lax.ppermute(near, axis, inside), from_far


SFC = ("y", "z", "core")


def on_device(adjoint, source, velocity, dissip, jacobian, cut_counts, cut_cell, face_angles, face_area, face_pressure,
              tri_owner, tri_local):
    parts = tuple(lax.axis_size(a) for a in SFC + ("blk",))
    n_y, n_z, n_c, n_x = parts
    _, size_x, size_y, size_z = adjoint.shape
    faces = cut_cell.shape[0]
    per_brick = faces // cut_counts.shape[0]
    f32 = jnp.float32
    smem = pl.BlockSpec(memory_space=pltpu.SMEM)
    vmem = pl.BlockSpec(memory_space=pltpu.VMEM)
    hbm = pl.BlockSpec(memory_space=pltpu.HBM)
    shape = jax.ShapeDtypeStruct
    owner = tri_owner.reshape(faces)
    jacobian = jnp.transpose(jacobian, (1, 0, 2))

    strip = shape((13, 16, size_z), f32)
    block = shape(adjoint.shape, f32)
    wall = shape((6, size_x, size_y, size_z), f32)
    dma = pltpu.SemaphoreType.DMA
    scratch = lambda *arrays: [pltpu.VMEM(a.shape, a.dtype) for a in arrays]
    padded = shape((5, size_x + 2, size_y, size_z), f32)
    edge = shape((5, size_x, size_z), f32)
    far_memory = lambda *arrays: [pltpu.with_memory_space_constraint(a, pltpu.HBM) for a in arrays]
    partial, walls, y_near_out, y_far_out, first, last = pl.pallas_call(
        functools.partial(first_kernel, per_brick),
        in_specs=[smem, smem] + [hbm] * 7,
        out_specs=[vmem] * 6,
        out_shape=[block, wall] + [strip] * 4,
        scratch_shapes=scratch(cut_cell, face_angles, face_area, padded, source, velocity, dissip)
        + [pltpu.VMEM((2,) + strip.shape, f32), dma((7,))],
        compiler_params=ROOM,
        name="first_step",
    )(jacobian, cut_counts, *far_memory(cut_cell, face_angles, face_area, adjoint, source, velocity, dissip))
    from_near, from_far = swap("blk", y_near_out, y_far_out)

    x_near_out, x_far_out = pl.pallas_call(
        second_kernel,
        in_specs=[smem] + [vmem] * 4,
        out_specs=[vmem] * 2,
        out_shape=[strip, strip],
        scratch_shapes=[pltpu.VMEM((2,) + strip.shape, f32)],
        compiler_params=SMALL,
        name="edge_rows",
    )(jacobian, from_near, from_far, first, last)
    x_near, x_far = swap(SFC, x_near_out, x_far_out)

    relaxed, message = pl.pallas_call(
        functools.partial(third_kernel, per_brick, parts),
        in_specs=[smem, smem] + [vmem] * 4 + [hbm] + [vmem] * 3 + [hbm] * 3 + [vmem] * 8,
        out_specs=[hbm, vmem],
        out_shape=[block, shape((n_y * n_c * n_x, 8 * n_z), f32)],
        scratch_shapes=scratch(padded, edge, edge, block, source, velocity, dissip, owner) + [dma((4,)), dma],
        compiler_params=ROOM,
        name="second_step",
    )(jacobian, cut_counts, cut_cell, face_angles, face_area, face_pressure, *far_memory(owner), tri_local, partial, walls,
      *far_memory(source, velocity, dissip), y_near_out, y_far_out, from_near, from_far, x_near_out, x_far_out, x_near, x_far)

    got = lax.all_to_all(message, ("y", "core", "blk"), split_axis=0, concat_axis=0, tiled=True)
    turned = pl.pallas_call(
        turn_kernel,
        in_specs=[vmem],
        out_specs=vmem,
        out_shape=shape((8 * n_z, 128), f32),
        compiler_params=SMALL,
        name="turn_words",
    )(got)
    got = lax.all_to_all(turned, "z", split_axis=0, concat_axis=0, tiled=True)
    sensitivity = pl.pallas_call(
        functools.partial(last_kernel, n_y * n_c * n_x),
        in_specs=[vmem],
        out_specs=vmem,
        out_shape=shape((3, TRI_DEV), f32),
        compiler_params=SMALL,
        name="sum_terms",
    )(got)
    return relaxed, sensitivity


def solution(mesh):
    n_sfc, n_blk = mesh.shape["sfc"], mesh.shape["blk"]
    n_z = min(16, n_sfc // 2)
    split = jax.sharding.Mesh(mesh.devices.reshape(n_sfc // (2 * n_z), n_z, 2, n_blk), SFC + ("blk",))
    grid = P(None, SFC, "blk", None)
    both = SFC + ("blk",)
    return jax.shard_map(
        on_device,
        mesh=split,
        in_specs=(grid, grid, grid, P(SFC, "blk", None), P(), P(both), P(both), P(None, both), P(both), P(both),
                  P(both, None), P(both)),
        out_specs=(grid, P(None, both)),
        check_vma=False,
    )
```

time: 86.7 us -> 73.7 us (0.85)
  local copies, waits for them, and re-layouts: 9.77 us -> 2.03 us
  Pallas kernels: 12.7 us -> 10.1 us
  blocking collectives: 41.5 us -> 39 us
  waiting for transfers between devices: 3.69 us -> 5.49 us
  starting transfers between devices: 17.2 us -> 15.9 us
    unnamed x49 -> x14, local copies, waits for them, and re-layouts: 9.77 us -> 2.03 us
    pallas_call x4, Pallas kernels: 9.08 us -> 6.16 us  [the longest x1 4.34 us: on_device(): pl.pallas_call(functools.partial(third_kernel, per_brick, parts), in_spec...]
    all_to_all x2, blocking collectives: 41.5 us -> 39 us  [the longest x1 19.6 us: on_device(): got = lax.all_to_all(turned, 'z', split_axis=0, concat_axis=0, tiled=True)]
    ppermute x4, waiting for transfers between devices: 3.69 us -> 5.49 us  [the longest x2 4.09 us: swap(): from_far = lax.ppermute(far, axis, across)]
    ppermute x4, starting transfers between devices: 17.2 us -> 15.9 us  [the longest x2 13.3 us: swap(): return (lax.ppermute(near, axis, inside), from_far)]
  transfers between devices with their start and end apart: 4 -> 4, of which waited for: 3 -> 2; matrix products, arithmetic and copies ran while one was open for 0% -> 0% of each run, Pallas kernels for 0% -> 0%
where the time goes in v1:
time: 73.7 us; the launch traced here: 73.3 us
  blocking collectives  39 us (53%)
  starting transfers between devices  15.9 us (22%)
  Pallas kernels  10.1 us (14%)
  waiting for transfers between devices  5.49 us (7%)
  local copies, waits for them, and re-layouts  2.03 us (3%)
  between operations  0.74 us (1%)
    all_to_all x1, blocking collectives, on_device(): got = lax.all_to_all(turned, 'z', split_axis=0, concat_axis=0, tiled=True)  19.6 us
    all_to_all x1, blocking collectives, on_device(): lax.all_to_all(message, ('y', 'core', 'blk'), split_axis=0, concat_axis=0...  19.4 us
    ppermute x2, starting transfers between devices, swap(): return (lax.ppermute(near, axis, inside), from_far)  13.3 us
    pallas_call x1, Pallas kernels, on_device(): pl.pallas_call(functools.partial(third_kernel, per_brick, parts), in_spec...  4.34 us
    ppermute x2, waiting for transfers between devices, swap(): from_far = lax.ppermute(far, axis, across)  4.09 us
    pallas_call x1, Pallas kernels, on_device(): pl.pallas_call(functools.partial(first_kernel, per_brick), in_specs=[smem...  3.97 us
    ppermute x2, starting transfers between devices, swap(): from_far = lax.ppermute(far, axis, across)  2.59 us
    unnamed x14, local copies, waits for them, and re-layouts  2.03 us
  transfers between devices with their start and end apart: 4, of which 2 were waited for; matrix products, arithmetic and copies ran while one was open for 0% of the time, Pallas kernels for 0%

profile of v1, /device:TPU:1, one launch (start us, length us, event | category | flops | bytes accessed | tf_op | source)
XLA Modules:
  0.0 73.3 jit_solution(14299394981886066618)
XLA Ops:
  0.6 0.0 copy-start.6
  0.6 0.6 copy-done.6
  1.3 0.7 copy-done
  2.0 4.0 %first_step.1 = (f32[5,16,16,128]{3,2,1,0:T(8,128)S(1)}, f32[6,16,16,128]{3,2,1,0:T(8,128)S(1)}, f32[13,16,128]{2,1,0:T(8,128)S(1)}, f32[13,16,128]{2,1,0:T(8,12...) custom-call(f32[5,3,5]{2,1,0:T(4,128)S(1)} %bitcast.10, s32[8]{0:T(128)S(1)} %copy-done.6, s32[512]{0:T(512)} %cell_ref.1, ...), custom_call_target="tpu_custom_call" | custom-call | tf_op jit(solution)/shard_map/first_step/pallas_call | solution.py:398
  6.0 3.9 %collective-permute-start = (f32[13,16,128]{2,1,0:T(8,128)S(1)}, f32[13,16,128]{2,1,0:T(8,128)S(1)}, u32[]{:S(2)}, u32[]{:S(2)}) collective-permute-start(f32[13,16,128]{2,1,0:T(8,128)S(1)} %get-tuple-element.14.y_own_near), channel_id=1, source_target_pairs={{0,1},{1,0},{2,3},{3,2},{4,5},{5,4},{6,7},{7,6},{8,9},{9,8},{10,11... | collective-permute-start | bytes 319496 | tf_op jit(solution)/shard_map/ppermute | solution.py:369
  9.9 0.7 collective-permute-start.1
  10.6 1.4 %collective-permute-done.from_near.y_near = f32[13,16,128]{2,1,0:T(8,128)S(1)} collective-permute-done((f32[13,16,128]{2,1,0:T(8,128)S(1)}, f32[13,16,128]{2,1,0:T(8,128)S(1)}, u32[]{:S(2)}, u32[]{:S(2)}) %collective-permute-start) | collective-permute-done | bytes 106528 | tf_op jit(solution)/shard_map/ppermute | solution.py:369
  12.0 0.0 collective-permute-done.1.from_far.y_far
  12.0 0.8 %edge_rows.1 = (f32[13,16,128]{2,1,0:T(8,128)S(1)}, f32[13,16,128]{2,1,0:T(8,128)S(1)}) custom-call(f32[5,3,5]{2,1,0:T(4,128)S(1)} %bitcast.11, f32[13,16,128]{2,1,0:T(8,128)S(1)} %collective-permute-done.from_near.y_near, f32[13,16,128]{2,1,0:T(8,128)S(1)} %collective-permute-done.1.from_far.y_far, f32[13,16,128]{2,1,0:T(8,128)S(1)} %get-tuple-element.16.first, ...), custom_call_target="tpu_custom_call" | custom-call | tf_op jit(solution)/shard_map/edge_rows/pallas_call | solution.py:410
  12.8 0.0 copy-start.1
  12.8 9.3 %collective-permute-start.2 = (f32[13,16,128]{2,1,0:T(8,128)S(1)}, f32[13,16,128]{2,1,0:T(8,128)S(1)}, u32[]{:S(2)}, u32[]{:S(2)}) collective-permute-start(f32[13,16,128]{2,1,0:T(8,128)S(1)} %get-tuple-element.18.x_own_near), channel_id=1, source_target_pairs={{0,4},{4,0},{8,12},{12,8},{16,20},{20,16},{24,28},{28,24},{32,36},... | collective-permute-start | bytes 319496 | tf_op jit(solution)/shard_map/ppermute | solution.py:369
  22.2 1.9 %collective-permute-start.3 = (f32[13,16,128]{2,1,0:T(8,128)S(1)}, f32[13,16,128]{2,1,0:T(8,128)S(1)}, u32[]{:S(2)}, u32[]{:S(2)}) collective-permute-start(f32[13,16,128]{2,1,0:T(8,128)S(1)} %get-tuple-element.19.x_own_far), channel_id=1, source_target_pairs={{4,8},{8,4},{12,16},{16,12},{20,24},{24,20},{28,32},{32,28},{36,40... | collective-permute-start | bytes 319496 | tf_op jit(solution)/shard_map/ppermute | solution.py:368
  24.1 0.0 collective-permute-done.2.x_near
  24.1 4.1 %collective-permute-done.3.x_far = f32[13,16,128]{2,1,0:T(8,128)S(1)} collective-permute-done((f32[13,16,128]{2,1,0:T(8,128)S(1)}, f32[13,16,128]{2,1,0:T(8,128)S(1)}, u32[]{:S(2)}, u32[]{:S(2)}) %collective-permute-start.3) | collective-permute-done | bytes 106528 | tf_op jit(solution)/shard_map/ppermute | solution.py:368
  28.2 0.0 copy-done.3
  28.2 0.0 copy-done.4
  28.2 0.0 copy-done.5
  28.2 0.0 copy-done.1
  28.2 0.7 copy-done.2
  28.9 4.3 %second_step.1 = (f32[5,16,16,128]{3,2,1,0:T(8,128)}, f32[32,128]{1,0:T(8,128)S(1)}) custom-call(f32[5,3,5]{2,1,0:T(4,128)S(1)} %bitcast.12, s32[8]{0:T(128)S(1)} %copy-done.6, s32[512]{0:T(512)S(1)} %copy-done.2, f32[2,512]{1,0:T(2,128)S(1)} %copy-done.1, f32[512]{0:T(512)S(1)} %copy-done.3, f32[512]{0:T(512)S(1)} %copy-done.4, s32[512]{0:T(512)} %bitcast.15, ...), custom_call_target="tpu_custom_call" | custom-call | tf_op jit(solution)/shard_map/second_step/pallas_call | solution.py:421
  33.2 19.4 %all_to_all.22 = f32[32,1,128]{2,1,0:T(1,128)S(1)} all-to-all(f32[32,1,128]{2,1,0:T(1,128)S(1)} %bitcast.14), channel_id=1, replica_groups=mesh['y'=4,'z'=16,'core'=2,'blk'=4] {'y','core','blk'}, dimensions={0} | all-to-all | bytes 32768 | tf_op jit(solution)/shard_map/all_to_all | solution.py:432
  52.7 0.1 turn_words.1
  52.8 19.6 %all_to_all.23 = f32[16,8,128]{2,1,0:T(8,128)S(1)} all-to-all(f32[16,8,128]{2,1,0:T(8,128)S(1)} %bitcast.8), channel_id=1, replica_groups=mesh['y'=4,'z'=16,'core'=2,'blk'=4] {'z'}, dimensions={0} | all-to-all | bytes 131072 | tf_op jit(solution)/shard_map/all_to_all | solution.py:441
  72.4 0.9 %sum_terms.1 = f32[3,256]{1,0:T(4,128)} custom-call(f32[128,128]{1,0:T(8,128)S(1)} %bitcast.9), custom_call_target="tpu_custom_call" | custom-call | tf_op jit(solution)/shard_map/sum_terms/pallas_call | solution.py:442
  (5 shorter events, 0.0 us)
Async XLA Ops:
  0.6 0.7 copy-start.6
  1.3 0.7 copy-start
  6.0 6.0 %collective-permute-start = (f32[13,16,128]{2,1,0:T(8,128)S(1)}, f32[13,16,128]{2,1,0:T(8,128)S(1)}, u32[]{:S(2)}, u32[]{:S(2)}) collective-permute-start(f32[13,16,128]{2,1,0:T(8,128)S(1)} %get-tuple-element.14.y_own_near), channel_id=1, source_target_pairs={{0,1},{1,0},{2,3},{3,2},{4,5},{5,4},{6,7},{7,6},{8,9},{9,8},{10,11... | collective-permute-start | bytes 319496 | tf_op jit(solution)/shard_map/ppermute | solution.py:369
  9.9 2.1 %collective-permute-start.1 = (f32[13,16,128]{2,1,0:T(8,128)S(1)}, f32[13,16,128]{2,1,0:T(8,128)S(1)}, u32[]{:S(2)}, u32[]{:S(2)}) collective-permute-start(f32[13,16,128]{2,1,0:T(8,128)S(1)} %get-tuple-element.15.y_own_far), channel_id=1, source_target_pairs={{1,2},{2,1},{5,6},{6,5},{9,10},{10,9},{13,14},{14,13},{17,18},{18,... | collective-permute-start | bytes 319496 | tf_op jit(solution)/shard_map/ppermute | solution.py:368
  12.0 16.2 %copy-start.3 = (f32[512]{0:T(512)S(1)}, f32[512]{0:T(512)}, u32[]{:S(2)}) copy-start(f32[512]{0:T(512)} %area_ref.1) | copy-start | bytes 6148
  12.0 16.2 %copy-start.4 = (f32[512]{0:T(512)S(1)}, f32[512]{0:T(512)}, u32[]{:S(2)}) copy-start(f32[512]{0:T(512)} %pressure_ref.1) | copy-start | bytes 6148
  12.0 16.2 %copy-start.5 = (s32[512]{0:T(512)S(1)}, s32[512]{0:T(512)}, u32[]{:S(2)}) copy-start(s32[512]{0:T(512)} %local_ref.1) | copy-start | bytes 6148
  12.8 15.4 %copy-start.1 = (f32[2,512]{1,0:T(2,128)S(1)}, f32[2,512]{1,0:T(2,128)}, u32[]{:S(2)}) copy-start(f32[2,512]{1,0:T(2,128)} %angle_ref.1) | copy-start | bytes 12292
  12.8 11.3 %collective-permute-start.2 = (f32[13,16,128]{2,1,0:T(8,128)S(1)}, f32[13,16,128]{2,1,0:T(8,128)S(1)}, u32[]{:S(2)}, u32[]{:S(2)}) collective-permute-start(f32[13,16,128]{2,1,0:T(8,128)S(1)} %get-tuple-element.18.x_own_near), channel_id=1, source_target_pairs={{0,4},{4,0},{8,12},{12,8},{16,20},{20,16},{24,28},{28,24},{32,36},... | collective-permute-start | bytes 319496 | tf_op jit(solution)/shard_map/ppermute | solution.py:369
  22.2 6.0 %collective-permute-start.3 = (f32[13,16,128]{2,1,0:T(8,128)S(1)}, f32[13,16,128]{2,1,0:T(8,128)S(1)}, u32[]{:S(2)}, u32[]{:S(2)}) collective-permute-start(f32[13,16,128]{2,1,0:T(8,128)S(1)} %get-tuple-element.19.x_own_far), channel_id=1, source_target_pairs={{4,8},{8,4},{12,16},{16,12},{20,24},{24,20},{28,32},{32,28},{36,40... | collective-permute-start | bytes 319496 | tf_op jit(solution)/shard_map/ppermute | solution.py:368
  28.2 0.7 copy-start.2

commit v2 on v1

--- a/solution.py
+++ b/solution.py
@@ -34,10 +34,9 @@
     return cosine[0:1] * across, sine[0:1] * across, sine[1:2]
 
 
-def cell_rows(cell, rows):
-    faces = cell.shape[1]
-    at = lax.broadcasted_iota(jnp.int32, (rows, faces), 0)
-    return jnp.where(at == cell // 16, 1.0, 0.0).astype(jnp.bfloat16)
+def one_hot(index, size):
+    at = lax.broadcasted_iota(jnp.int32, (size, index.shape[1]), 0)
+    return jnp.where(at == index, 1.0, 0.0).astype(jnp.bfloat16)
 
 
 def cell_depth(cell, per_brick):
@@ -124,7 +123,7 @@
 
 
 def first_kernel(per_brick, jac, counts, cell_hbm, angle_hbm, area_hbm, adjoint_hbm, source_hbm, velocity_hbm, dissip_hbm,
-                 partial, walls, near_out, far_out, first_out, last_out,
+                 partial, walls, near_out, far_out, near_end, far_end, face_out,
                  cell_ref, angle_ref, area_ref, field, source, velocity, dissip, edges, sems):
     size_x, size_y, size_z = dissip.shape
     copies = start_all([(cell_hbm, cell_ref), (angle_hbm, angle_ref), (area_hbm, area_ref),
@@ -141,10 +140,11 @@
     area = area_ref[...].reshape(1, faces)
     normal = face_normals(angle_ref[...])
     weight = face_weight(counts, area, per_brick)
-    rows = cell_rows(cell, size_x * size_y)
+    rows = one_hot(cell // 16, size_x * size_y)
     depth = cell_depth(cell, per_brick)
     at = lax.broadcasted_iota(jnp.int32, (size_z, faces), 0) == depth
     hot = jnp.where(at, 1.0, 0.0).astype(jnp.bfloat16)
+    face_out[...] = jnp.concatenate([*normal, weight, jnp.zeros((4, faces), jnp.float32)], axis=0)
     rows = jnp.concatenate([rows, rows], axis=1)
     pairs = ((0, 0), (0, 1), (0, 2), (1, 1), (1, 2), (2, 2))
     for m in range(0, 6, 2):
@@ -179,7 +179,8 @@
     lax.fori_loop(0, size_x, step, 0, unroll=2)
     near_out[...] = edges[0]
     far_out[...] = edges[1]
-    for out, x in ((first_out, 0), (last_out, size_x - 1)):
+    odd = lax.axis_index("core")
+    for out, x in ((near_end, (1 - odd) * (size_x - 1)), (far_end, odd * (size_x - 1))):
         for c in range(5):
             out[c] = field[c, x + 1]
             out[5 + c] = partial[c, x]
@@ -188,126 +189,36 @@
         out[12] = velocity[1, x].astype(jnp.float32)
 
 
-def second_kernel(jac, from_near, from_far, first, last, near_out, far_out, both):
-    rows, lanes = first.shape[1:]
+def edge_kernel(is_near, jac, from_near, from_far, mine, out):
+    rows, lanes = mine.shape[1:]
     at_y = lax.broadcasted_iota(jnp.int32, (rows, lanes), 0)
-    odd = lax.axis_index("blk") % 2 == 1
-    side = 1 - lax.axis_index("core")
-    for mine, place, x in ((first, side, 0), (last, 1 - side, from_near.shape[1] - 1)):
-        speed_y = mine[12]
-        damping = mine[11]
-        near = [from_near[c, x:x + 1, :] for c in range(5)]
-        far = [from_far[c, x:x + 1, :] for c in range(5)]
-        low = [jnp.where(odd, a, b) for a, b in zip(near, far)]
-        high = [jnp.where(odd, b, a) for a, b in zip(near, far)]
-        add_low = coupled(jac, 1, 1.0, speed_y[0:1], damping[0:1], low)
-        add_high = coupled(jac, 1, -1.0, speed_y[rows - 1:rows], damping[rows - 1:rows], high)
-        for c in range(5):
-            both[place, c] = mine[c]
-            fixed = mine[5 + c]
-            fixed = fixed + jnp.where(at_y == 0, add_low[c], 0.0)
-            both[place, 5 + c] = fixed + jnp.where(at_y == rows - 1, add_high[c], 0.0)
-        both[place, 10] = mine[10]
-        both[place, 11] = damping
-        both[place, 12] = jnp.concatenate(low + high + [jnp.zeros((rows - 10, lanes), jnp.float32)], axis=0)
-    near_out[...] = both[0]
-    far_out[...] = both[1]
-
-
-def third_kernel(per_brick, parts, jac, counts, cell_ref, angle_ref, area_ref, pressure_ref, owner_hbm, local_ref,
-                 partial, walls, source_hbm, velocity_hbm, dissip_hbm, y_own_near, y_own_far, y_near, y_far,
-                 x_own_near, x_own_far, x_near, x_far, relaxed_hbm, message,
-                 field, edge_low, edge_high, relaxed, source, velocity, dissip, owner_ref, sems, out_sem):
-    copies = start_all([(velocity_hbm, velocity), (dissip_hbm, dissip), (source_hbm, source), (owner_hbm, owner_ref)], sems)
+    odd_y = lax.axis_index("blk") % 2 == 1
+    last = (lax.axis_index("core") == 1) != is_near
+    end = from_near.shape[1] - 1
+    near = [jnp.where(last, from_near[c, end:end + 1, :], from_near[c, 0:1, :]) for c in range(5)]
+    far = [jnp.where(last, from_far[c, end:end + 1, :], from_far[c, 0:1, :]) for c in range(5)]
+    low = [jnp.where(odd_y, a, b) for a, b in zip(near, far)]
+    high = [jnp.where(odd_y, b, a) for a, b in zip(near, far)]
+    speed_y = mine[12]
+    damping = mine[11]
+    add_low = coupled(jac, 1, 1.0, speed_y[0:1], damping[0:1], low)
+    add_high = coupled(jac, 1, -1.0, speed_y[rows - 1:rows], damping[rows - 1:rows], high)
+    for c in range(5):
+        out[c] = mine[c]
+        fixed = mine[5 + c]
+        fixed = fixed + jnp.where(at_y == 0, add_low[c], 0.0)
+        out[5 + c] = fixed + jnp.where(at_y == rows - 1, add_high[c], 0.0)
+    out[10] = mine[10]
+    out[11] = damping
+    out[12] = jnp.concatenate(low + high + [jnp.zeros((rows - 10, lanes), jnp.float32)], axis=0)
+
+
+def plan_kernel(per_brick, parts, after, face, cell_ref, pressure_ref, owner_ref, local_ref, plan):
+    del after
     faces = cell_ref.shape[0]
-    size_x, size_y, size_z = dissip.shape
-    for c in range(5):
-        field[c, 1:1 + size_x] = partial[c]
-    odd_y = lax.axis_index("blk") % 2 == 1
-    odd_x = lax.axis_index("core") == 1
-
-    class Sorted:
-        def __init__(self, odd, when_odd, when_even):
-            self.odd, self.when_odd, self.when_even = odd, when_odd, when_even
-
-        def __getitem__(self, at):
-            return jnp.where(self.odd, self.when_odd[at], self.when_even[at])
-
-    y_low, y_high = Sorted(odd_y, y_near, y_far), Sorted(odd_y, y_far, y_near)
-    y_own_low, y_own_high = Sorted(odd_y, y_own_near, y_own_far), Sorted(odd_y, y_own_far, y_own_near)
-    x_low, x_high = Sorted(odd_x, x_near, x_far), Sorted(odd_x, x_far, x_near)
-    x_own_low, x_own_high = Sorted(odd_x, x_own_near, x_own_far), Sorted(odd_x, x_own_far, x_own_near)
-    grab = lambda ref: [ref[c] for c in range(5)]
-    add = coupled(jac, 0, 1.0, x_own_low[10], x_own_low[11], grab(x_low))
-    for c in range(5):
-        field[c, 1] = field[c, 1] + add[c]
-    add = coupled(jac, 0, -1.0, x_own_high[10], x_own_high[11], grab(x_high))
-    for c in range(5):
-        field[c, size_x] = field[c, size_x] + add[c]
-    add_low = coupled(jac, 1, 1.0, y_own_low[10], y_own_low[11], grab(y_low))
-    add_high = coupled(jac, 1, -1.0, y_own_high[10], y_own_high[11], grab(y_high))
-    for c in range(5):
-        for x in range(size_x):
-            field[c, 1 + x, 0:1, :] = field[c, 1 + x, 0:1, :] + add_low[c][x:x + 1]
-            field[c, 1 + x, size_y - 1:size_y, :] = field[c, 1 + x, size_y - 1:size_y, :] + add_high[c][x:x + 1]
-    add = coupled(jac, 0, -1.0, x_low[10], x_low[11], grab(x_own_low))
-    for c in range(5):
-        field[c, 0] = x_low[5 + c] + add[c]
-    add = coupled(jac, 0, 1.0, x_high[10], x_high[11], grab(x_own_high))
-    for c in range(5):
-        field[c, size_x + 1] = x_high[5 + c] + add[c]
-    at_x = lax.broadcasted_iota(jnp.int32, (size_x, size_z), 0)
-    for edge, theirs, own, side, corner in ((edge_low, y_low, y_own_low, -1.0, 0), (edge_high, y_high, y_own_high, 1.0, 5)):
-        add = coupled(jac, 1, side, theirs[10], theirs[11], grab(own))
-        speed = theirs[12]
-        damping = theirs[11]
-        first = [x_low[12, corner + c:corner + c + 1, :] for c in range(5)]
-        last = [x_high[12, corner + c:corner + c + 1, :] for c in range(5)]
-        add_first = coupled(jac, 0, 1.0, speed[0:1], damping[0:1], first)
-        add_last = coupled(jac, 0, -1.0, speed[size_x - 1:size_x], damping[size_x - 1:size_x], last)
-        for c in range(5):
-            value = theirs[5 + c] + add[c]
-            value = value + jnp.where(at_x == 0, add_first[c], 0.0)
-            edge[c] = value + jnp.where(at_x == size_x - 1, add_last[c], 0.0)
-
-    def step(x, carry):
-        here = [field[c, x + 1] for c in range(5)]
-        below = [field[c, x] for c in range(5)]
-        above = [field[c, x + 2] for c in range(5)]
-        lows = [edge_low[c, pl.ds(x, 1), :] for c in range(5)]
-        highs = [edge_high[c, pl.ds(x, 1), :] for c in range(5)]
-        src = [source[c, x] for c in range(5)]
-        speed = [velocity[d, x].astype(jnp.float32) for d in range(3)]
-        damping = dissip[x].astype(jnp.float32)
-        sym = [walls[m, x] for m in range(6)]
-        wall = [[sym[SYM[a][b]] for b in range(3)] for a in range(3)]
-        out = relax_row(jac, here, below, above, lows, highs, src, speed, damping, wall)
-        for c in range(5):
-            relaxed[c, x] = out[c]
-        return carry
-
-    wait_all(copies)
-    lax.fori_loop(0, size_x, step, 0, unroll=2)
-    done = pltpu.make_async_copy(relaxed, relaxed_hbm, out_sem)
-    done.start()
-
     cell = cell_ref[...].reshape(1, faces)
-    area = area_ref[...].reshape(1, faces)
-    normal = face_normals(angle_ref[...])
-    weight = face_weight(counts, area, per_brick)
-    rows = cell_rows(cell, size_x * size_y)
-    depth = cell_depth(cell, per_brick)
-    turned = []
-    for c in range(3):
-        high, low = halves(relaxed[1 + c].reshape(size_x * size_y, size_z).T)
-        turned.append(jnp.concatenate([high, low], axis=1))
-    picked = jnp.dot(jnp.concatenate(turned, axis=0), jnp.concatenate([rows, rows], axis=0),
-                     preferred_element_type=jnp.float32)
-    along = normal[0] * picked[:size_z] + normal[1] * picked[size_z:2 * size_z] + normal[2] * picked[2 * size_z:]
-    at = lax.broadcasted_iota(jnp.int32, (size_z, faces), 0) == depth
-    project = jnp.sum(jnp.where(at, along, 0.0), axis=0, keepdims=True)
-    scale = pressure_ref[...].reshape(1, faces) * weight * project
     owner = owner_ref[...].reshape(1, faces)
+    strength = pressure_ref[...].reshape(1, faces) * face[3:4]
     label = local_ref[...].reshape(1, faces).astype(jnp.float32)
     block = min(faces, 128)
     number = owner.astype(jnp.float32)
@@ -323,14 +234,107 @@
         ranks.append(jnp.sum(same, axis=0, keepdims=True))
     rank = jnp.concatenate(ranks, axis=1)
     n_y, n_z, n_c, n_x = parts
+    at_x, at_c, at_z, at_y = owner % n_x, owner // n_x % n_c, owner // (n_x * n_c) % n_z, owner // (n_x * n_c * n_z)
+    whole = [cell // 16, cell_depth(cell, per_brick), at_z, (at_y * n_c + at_c) * n_x + at_x]
+    rows = [face[0:1], face[1:2], face[2:3], strength, rank, label] + [w.astype(jnp.float32) for w in whole]
+    plan[...] = jnp.concatenate(rows + [jnp.zeros((16 - len(rows), faces), jnp.float32)], axis=0)
+
+
+def third_kernel(parts, jac, plan, partial, walls, source, velocity, dissip, y_own_near, y_own_far, y_near, y_far,
+                 x_own_near, x_own_far, x_near, x_far, relaxed_hbm, message,
+                 field, edge_low, edge_high, relaxed, out_sem):
+    faces = plan.shape[1]
+    size_x, size_y, size_z = dissip.shape
+    for c in range(5):
+        field[c, 1:1 + size_x] = partial[c]
+    odd_y = lax.axis_index("blk") % 2 == 1
+    odd_x = lax.axis_index("core") == 1
+
+    class Sorted:
+        def __init__(self, odd, when_odd, when_even):
+            self.odd, self.when_odd, self.when_even = odd, when_odd, when_even
+
+        def __getitem__(self, at):
+            return jnp.where(self.odd, self.when_odd[at], self.when_even[at])
+
+    y_low, y_high = Sorted(odd_y, y_near, y_far), Sorted(odd_y, y_far, y_near)
+    y_own_low, y_own_high = Sorted(odd_y, y_own_near, y_own_far), Sorted(odd_y, y_own_far, y_own_near)
+    x_low, x_high = Sorted(odd_x, x_near, x_far), Sorted(odd_x, x_far, x_near)
+    x_own_low, x_own_high = Sorted(odd_x, x_own_near, x_own_far), Sorted(odd_x, x_own_far, x_own_near)
+    grab = lambda ref: [ref[c] for c in range(5)]
+    add = coupled(jac, 0, 1.0, x_own_low[10], x_own_low[11], grab(x_low))
+    for c in range(5):
+        field[c, 1] = field[c, 1] + add[c]
+    add = coupled(jac, 0, -1.0, x_own_high[10], x_own_high[11], grab(x_high))
+    for c in range(5):
+        field[c, size_x] = field[c, size_x] + add[c]
+    add_low = coupled(jac, 1, 1.0, y_own_low[10], y_own_low[11], grab(y_low))
+    add_high = coupled(jac, 1, -1.0, y_own_high[10], y_own_high[11], grab(y_high))
+    for c in range(5):
+        for x in range(size_x):
+            field[c, 1 + x, 0:1, :] = field[c, 1 + x, 0:1, :] + add_low[c][x:x + 1]
+            field[c, 1 + x, size_y - 1:size_y, :] = field[c, 1 + x, size_y - 1:size_y, :] + add_high[c][x:x + 1]
+    add = coupled(jac, 0, -1.0, x_low[10], x_low[11], grab(x_own_low))
+    for c in range(5):
+        field[c, 0] = x_low[5 + c] + add[c]
+    add = coupled(jac, 0, 1.0, x_high[10], x_high[11], grab(x_own_high))
+    for c in range(5):
+        field[c, size_x + 1] = x_high[5 + c] + add[c]
+    at_x = lax.broadcasted_iota(jnp.int32, (size_x, size_z), 0)
+    for edge, theirs, own, side, corner in ((edge_low, y_low, y_own_low, -1.0, 0), (edge_high, y_high, y_own_high, 1.0, 5)):
+        add = coupled(jac, 1, side, theirs[10], theirs[11], grab(own))
+        speed = theirs[12]
+        damping = theirs[11]
+        first = [x_low[12, corner + c:corner + c + 1, :] for c in range(5)]
+        last = [x_high[12, corner + c:corner + c + 1, :] for c in range(5)]
+        add_first = coupled(jac, 0, 1.0, speed[0:1], damping[0:1], first)
+        add_last = coupled(jac, 0, -1.0, speed[size_x - 1:size_x], damping[size_x - 1:size_x], last)
+        for c in range(5):
+            value = theirs[5 + c] + add[c]
+            value = value + jnp.where(at_x == 0, add_first[c], 0.0)
+            edge[c] = value + jnp.where(at_x == size_x - 1, add_last[c], 0.0)
+
+    def step(x, carry):
+        here = [field[c, x + 1] for c in range(5)]
+        below = [field[c, x] for c in range(5)]
+        above = [field[c, x + 2] for c in range(5)]
+        lows = [edge_low[c, pl.ds(x, 1), :] for c in range(5)]
+        highs = [edge_high[c, pl.ds(x, 1), :] for c in range(5)]
+        src = [source[c, x] for c in range(5)]
+        speed = [velocity[d, x].astype(jnp.float32) for d in range(3)]
+        damping = dissip[x].astype(jnp.float32)
+        sym = [walls[m, x] for m in range(6)]
+        wall = [[sym[SYM[a][b]] for b in range(3)] for a in range(3)]
+        out = relax_row(jac, here, below, above, lows, highs, src, speed, damping, wall)
+        for c in range(5):
+            relaxed[c, x] = out[c]
+        return carry
+
+    lax.fori_loop(0, size_x, step, 0, unroll=2)
+    done = pltpu.make_async_copy(relaxed, relaxed_hbm, out_sem)
+    done.start()
+
+    normal = [plan[c:c + 1] for c in range(3)]
+    strength, rank, label = plan[3:4], plan[4:5], plan[5:6]
+    cell_row, depth, at_z, target_row = [plan[i:i + 1].astype(jnp.int32) for i in range(6, 10)]
+    rows = one_hot(cell_row, size_x * size_y)
+    turned = []
+    for c in range(3):
+        high, low = halves(relaxed[1 + c].reshape(size_x * size_y, size_z).T)
+        turned.append(jnp.concatenate([high, low], axis=1))
+    picked = jnp.dot(jnp.concatenate(turned, axis=0), jnp.concatenate([rows, rows], axis=0),
+                     preferred_element_type=jnp.float32)
+    along = normal[0] * picked[:size_z] + normal[1] * picked[size_z:2 * size_z] + normal[2] * picked[2 * size_z:]
+    at = lax.broadcasted_iota(jnp.int32, (size_z, faces), 0) == depth
+    project = jnp.sum(jnp.where(at, along, 0.0), axis=0, keepdims=True)
+    scale = strength * project
+    n_y, n_z, n_c, n_x = parts
     words = [normal[0] * scale, normal[1] * scale, normal[2] * scale, label]
     pair = [jnp.where(rank == float(j), w, 0.0) for j in range(2) for w in words]
     high, low = halves(jnp.concatenate(pair * n_z, axis=0))
-    at_x, at_c, at_z, at_y = owner % n_x, owner // n_x % n_c, owner // (n_x * n_c) % n_z, owner // (n_x * n_c * n_z)
     lane = lax.broadcasted_iota(jnp.int32, (8 * n_z, faces), 0)
     hot = jnp.where(lane // 8 == at_z, 1.0, 0.0).astype(jnp.bfloat16)
-    target = lax.broadcasted_iota(jnp.int32, (n_y * n_c * n_x, faces), 0)
-    target = jnp.where(target == (at_y * n_c + at_c) * n_x + at_x, 1.0, 0.0).astype(jnp.bfloat16)
+    target = one_hot(target_row, n_y * n_c * n_x)
     message[...] = dot_last(jnp.concatenate([target, target], axis=1),
                             jnp.concatenate([hot * high, hot * low], axis=1))
     done.wait()
@@ -395,39 +399,52 @@
     padded = shape((5, size_x + 2, size_y, size_z), f32)
     edge = shape((5, size_x, size_z), f32)
     far_memory = lambda *arrays: [pltpu.with_memory_space_constraint(a, pltpu.HBM) for a in arrays]
-    partial, walls, y_near_out, y_far_out, first, last = pl.pallas_call(
+    far_memory = lambda *arrays: [pltpu.with_memory_space_constraint(a, pltpu.HBM) for a in arrays]
+    partial, walls, y_near_out, y_far_out, near_end, far_end, face = pl.pallas_call(
         functools.partial(first_kernel, per_brick),
         in_specs=[smem, smem] + [hbm] * 7,
-        out_specs=[vmem] * 6,
-        out_shape=[block, wall] + [strip] * 4,
+        out_specs=[vmem] * 7,
+        out_shape=[block, wall] + [strip] * 4 + [shape((8, faces), f32)],
         scratch_shapes=scratch(cut_cell, face_angles, face_area, padded, source, velocity, dissip)
         + [pltpu.VMEM((2,) + strip.shape, f32), dma((7,))],
         compiler_params=ROOM,
         name="first_step",
-    )(jacobian, cut_counts, *far_memory(cut_cell, face_angles, face_area, adjoint, source, velocity, dissip))
+    )(*far_memory(jacobian, cut_counts, cut_cell, face_angles, face_area, adjoint, source, velocity, dissip))
     from_near, from_far = swap("blk", y_near_out, y_far_out)
 
-    x_near_out, x_far_out = pl.pallas_call(
-        second_kernel,
-        in_specs=[smem] + [vmem] * 4,
-        out_specs=[vmem] * 2,
-        out_shape=[strip, strip],
-        scratch_shapes=[pltpu.VMEM((2,) + strip.shape, f32)],
+    def edge_rows(is_near, end):
+        return pl.pallas_call(
+            functools.partial(edge_kernel, is_near),
+            in_specs=[smem] + [vmem] * 3,
+            out_specs=vmem,
+            out_shape=strip,
+            compiler_params=SMALL,
+            name="edge_rows",
+        )(jacobian, from_near, from_far, end)
+
+    x_far_out = edge_rows(False, far_end)
+    x_near_out = edge_rows(True, near_end)
+    x_near, x_far = swap(SFC, x_near_out, x_far_out)
+
+    plan = pl.pallas_call(
+        functools.partial(plan_kernel, per_brick, parts),
+        in_specs=[pl.BlockSpec(memory_space=pl.ANY)] + [vmem] * 5,
+        out_specs=vmem,
+        out_shape=shape((16, faces), f32),
         compiler_params=SMALL,
-        name="edge_rows",
-    )(jacobian, from_near, from_far, first, last)
-    x_near, x_far = swap(SFC, x_near_out, x_far_out)
+        name="face_plan",
+    )(x_near_out, face, cut_cell, face_pressure, owner, tri_local)
 
     relaxed, message = pl.pallas_call(
-        functools.partial(third_kernel, per_brick, parts),
-        in_specs=[smem, smem] + [vmem] * 4 + [hbm] + [vmem] * 3 + [hbm] * 3 + [vmem] * 8,
+        functools.partial(third_kernel, parts),
+        in_specs=[smem] + [vmem] * 14,
         out_specs=[hbm, vmem],
         out_shape=[block, shape((n_y * n_c * n_x, 8 * n_z), f32)],
-        scratch_shapes=scratch(padded, edge, edge, block, source, velocity, dissip, owner) + [dma((4,)), dma],
+        scratch_shapes=scratch(padded, edge, edge, block) + [dma],
         compiler_params=ROOM,
         name="second_step",
-    )(jacobian, cut_counts, cut_cell, face_angles, face_area, face_pressure, *far_memory(owner), tri_local, partial, walls,
-      *far_memory(source, velocity, dissip), y_near_out, y_far_out, from_near, from_far, x_near_out, x_far_out, x_near, x_far)
+    )(jacobian, plan, partial, walls, source, velocity, dissip, y_near_out, y_far_out, from_near, from_far,
+      x_near_out, x_far_out, x_near, x_far)
 
     got = lax.all_to_all(message, ("y", "core", "blk"), split_axis=0, concat_axis=0, tiled=True)
     turned = pl.pallas_call(

time: 73.7 us -> 69.6 us (0.944)
  waiting for transfers between devices: 5.49 us -> 2.12 us
  local copies, waits for them, and re-layouts: 2.03 us -> 0.05 us
  blocking collectives: 39 us -> 40.8 us
  starting transfers between devices: 15.9 us -> 14.8 us
    ppermute x2, starting transfers between devices: 13.3 us -> 8.59 us  [swap(): return (lax.ppermute(near, axis, inside), from_far)]
    ppermute x2, waiting for transfers between devices: 4.09 us -> 0.01 us  [swap(): from_far = lax.ppermute(far, axis, across)]
    ppermute x2, starting transfers between devices: 2.59 us -> 6.17 us  [swap(): from_far = lax.ppermute(far, axis, across)]
    unnamed x14 -> x16, local copies, waits for them, and re-layouts: 2.03 us -> 0.05 us
    all_to_all x1, blocking collectives: 19.4 us -> 20.7 us  [on_device(): lax.all_to_all(message, ('y', 'core', 'blk'), split_axis=0, concat_axis=0...]
    pallas_call x2 -> x4, Pallas kernels: 5.13 us -> 5.57 us  [the longest x1 3.92 us: on_device(): pl.pallas_call(functools.partial(third_kernel, parts), in_specs=[smem] +...]
  transfers between devices with their start and end apart: 4 -> 4, of which waited for: 2 -> 2; matrix products, arithmetic and copies ran while one was open for 0% -> 0% of each run, Pallas kernels for 0% -> 1%
where the time goes in v2:
time: 69.6 us; the launch traced here: 69.3 us
  blocking collectives  40.8 us (59%)
  starting transfers between devices  14.8 us (21%)
  Pallas kernels  10.8 us (16%)
  waiting for transfers between devices  2.12 us (3%)
  between operations  0.81 us (1%)
    all_to_all x1, blocking collectives, on_device(): lax.all_to_all(message, ('y', 'core', 'blk'), split_axis=0, concat_axis=0...  20.7 us
    all_to_all x1, blocking collectives, on_device(): got = lax.all_to_all(turned, 'z', split_axis=0, concat_axis=0, tiled=True)  20.1 us
    ppermute x2, starting transfers between devices, swap(): return (lax.ppermute(near, axis, inside), from_far)  8.59 us
    ppermute x2, starting transfers between devices, swap(): from_far = lax.ppermute(far, axis, across)  6.17 us
    pallas_call x1, Pallas kernels, on_device(): pl.pallas_call(functools.partial(first_kernel, per_brick), in_specs=[smem...  4.2 us
    pallas_call x1, Pallas kernels, on_device(): pl.pallas_call(functools.partial(third_kernel, parts), in_specs=[smem] +...  3.92 us
    ppermute x2, waiting for transfers between devices, swap(): return (lax.ppermute(near, axis, inside), from_far)  2.12 us
    pallas_call x2, Pallas kernels, edge_rows(): pl.pallas_call(functools.partial(edge_kernel, is_near), in_specs=[smem] +...  1.5 us
  transfers between devices with their start and end apart: 4, of which 2 were waited for; matrix products, arithmetic and copies ran while one was open for 0% of the time, Pallas kernels for 1%

profile of v2, /device:TPU:1, one launch (start us, length us, event | category | flops | bytes accessed | tf_op | source)
XLA Modules:
  0.0 69.3 jit_solution(4142619517817811788)
XLA Ops:
  0.6 4.2 %first_step.1 = (f32[5,16,16,128]{3,2,1,0:T(8,128)S(1)}, f32[6,16,16,128]{3,2,1,0:T(8,128)S(1)}, f32[13,16,128]{2,1,0:T(8,128)S(1)}, f32[13,16,128]{2,1,0:T(8,12...) custom-call(f32[5,3,5]{2,1,0:T(4,128)} %bitcast.10, s32[8]{0:T(128)} %counts.1, ...), custom_call_target="tpu_custom_call" | custom-call | tf_op jit(solution)/shard_map/first_step/pallas_call | solution.py:403
  4.8 0.0 copy-start
  4.9 4.1 %collective-permute-start = (f32[13,16,128]{2,1,0:T(8,128)S(1)}, f32[13,16,128]{2,1,0:T(8,128)S(1)}, u32[]{:S(2)}, u32[]{:S(2)}) collective-permute-start(f32[13,16,128]{2,1,0:T(8,128)S(1)} %get-tuple-element.11.y_own_near), channel_id=1, source_target_pairs={{0,1},{1,0},{2,3},{3,2},{4,5},{5,4},{6,7},{7,6},{8,9},{9,8},{10,11... | collective-permute-start | bytes 319496 | tf_op jit(solution)/shard_map/ppermute | solution.py:373
  8.9 0.7 collective-permute-start.1
  9.6 1.4 %collective-permute-done.from_near.y_near = f32[13,16,128]{2,1,0:T(8,128)S(1)} collective-permute-done((f32[13,16,128]{2,1,0:T(8,128)S(1)}, f32[13,16,128]{2,1,0:T(8,128)S(1)}, u32[]{:S(2)}, u32[]{:S(2)}) %collective-permute-start) | collective-permute-done | bytes 106528 | tf_op jit(solution)/shard_map/ppermute | solution.py:373
  11.0 0.0 collective-permute-done.1.from_far.y_far
  11.0 0.7 %edge_rows.3.x_own_far = f32[13,16,128]{2,1,0:T(8,128)S(1)} custom-call(f32[5,3,5]{2,1,0:T(4,128)S(1)} %bitcast.11, f32[13,16,128]{2,1,0:T(8,128)S(1)} %collective-permute-done.from_near.y_near, f32[13,16,128]{2,1,0:T(8,128)S(1)} %collective-permute-done.1.from_far.y_far, f32[13,16,128]{2,1,0:T(8,128)S(1)} %get-tuple-element.17.mine), custom_call_target="tpu_custom_call" | custom-call | tf_op jit(solution)/shard_map/edge_rows/pallas_call | solution.py:416
  11.8 5.5 %collective-permute-start.3 = (f32[13,16,128]{2,1,0:T(8,128)S(1)}, f32[13,16,128]{2,1,0:T(8,128)S(1)}, u32[]{:S(2)}, u32[]{:S(2)}) collective-permute-start(f32[13,16,128]{2,1,0:T(8,128)S(1)} %edge_rows.3.x_own_far), channel_id=1, source_target_pairs={{4,8},{8,4},{12,16},{16,12},{20,24},{24,20},{28,32},{32,28},{36,40... | collective-permute-start | bytes 319496 | tf_op jit(solution)/shard_map/ppermute | solution.py:372
  17.3 0.0 copy-start.5
  17.3 0.0 copy-start.6
  17.3 0.0 copy-start.7
  17.3 0.0 copy-start.1
  17.3 0.7 %edge_rows.2.after.x_own_near = f32[13,16,128]{2,1,0:T(8,128)S(1)} custom-call(f32[5,3,5]{2,1,0:T(4,128)S(1)} %bitcast.12, f32[13,16,128]{2,1,0:T(8,128)S(1)} %collective-permute-done.from_near.y_near, f32[13,16,128]{2,1,0:T(8,128)S(1)} %collective-permute-done.1.from_far.y_far, f32[13,16,128]{2,1,0:T(8,128)S(1)} %get-tuple-element.13.mine), custom_call_target="tpu_custom_call" | custom-call | tf_op jit(solution)/shard_map/edge_rows/pallas_call | solution.py:416
  18.1 0.0 copy-start.4
  18.1 4.5 %collective-permute-start.2 = (f32[13,16,128]{2,1,0:T(8,128)S(1)}, f32[13,16,128]{2,1,0:T(8,128)S(1)}, u32[]{:S(2)}, u32[]{:S(2)}) collective-permute-start(f32[13,16,128]{2,1,0:T(8,128)S(1)} %edge_rows.2.after.x_own_near), channel_id=1, source_target_pairs={{0,4},{4,0},{8,12},{12,8},{16,20},{20,16},{24,28},{28,24},{32,36},... | collective-permute-start | bytes 319496 | tf_op jit(solution)/shard_map/ppermute | solution.py:373
  22.7 0.0 copy-start.2
  22.7 0.2 face_plan.1.plan
  22.8 0.0 collective-permute-done.3.x_far
  22.9 0.7 %collective-permute-done.2.x_near = f32[13,16,128]{2,1,0:T(8,128)S(1)} collective-permute-done((f32[13,16,128]{2,1,0:T(8,128)S(1)}, f32[13,16,128]{2,1,0:T(8,128)S(1)}, u32[]{:S(2)}, u32[]{:S(2)}) %collective-permute-start.2) | collective-permute-done | bytes 106528 | tf_op jit(solution)/shard_map/ppermute | solution.py:373
  23.6 3.9 %second_step.1 = (f32[5,16,16,128]{3,2,1,0:T(8,128)}, f32[32,128]{1,0:T(8,128)S(1)}) custom-call(f32[5,3,5]{2,1,0:T(4,128)S(1)} %bitcast.13, f32[16,512]{1,0:T(8,128)S(1)} %face_plan.1.plan, f32[5,16,16,128]{3,2,1,0:T(8,128)S(1)} %get-tuple-element.15.partial, f32[6,16,16,128]{3,2,1,0:T(8,128)S(1)} %get-tuple-element.16.walls, ...), custom_call_target="tpu_custom_call" | custom-call | tf_op jit(solution)/shard_map/second_step/pallas_call | solution.py:438
  27.5 20.7 %all_to_all.22 = f32[32,1,128]{2,1,0:T(1,128)S(1)} all-to-all(f32[32,1,128]{2,1,0:T(1,128)S(1)} %bitcast.15), channel_id=1, replica_groups=mesh['y'=4,'z'=16,'core'=2,'blk'=4] {'y','core','blk'}, dimensions={0} | all-to-all | bytes 32768 | tf_op jit(solution)/shard_map/all_to_all | solution.py:449
  48.2 0.1 turn_words.1
  48.3 20.1 %all_to_all.23 = f32[16,8,128]{2,1,0:T(8,128)S(1)} all-to-all(f32[16,8,128]{2,1,0:T(8,128)S(1)} %bitcast.8), channel_id=1, replica_groups=mesh['y'=4,'z'=16,'core'=2,'blk'=4] {'z'}, dimensions={0} | all-to-all | bytes 131072 | tf_op jit(solution)/shard_map/all_to_all | solution.py:458
  68.4 0.9 %sum_terms.1 = f32[3,256]{1,0:T(4,128)} custom-call(f32[128,128]{1,0:T(8,128)S(1)} %bitcast.9), custom_call_target="tpu_custom_call" | custom-call | tf_op jit(solution)/shard_map/sum_terms/pallas_call | solution.py:459
  (9 shorter events, 0.0 us)
Async XLA Ops:
  0.6 10.4 %copy-start.3 = (f32[3,5,5]{2,0,1:T(4,128)S(1)}, f32[3,5,5]{2,0,1:T(4,128)}, u32[]{:S(2)}) copy-start(f32[3,5,5]{2,0,1:T(4,128)} %param.16) | copy-start | bytes 904
  4.8 18.7 %copy-start = (f32[5,16,16,128]{3,2,1,0:T(8,128)S(1)}, f32[5,16,16,128]{3,2,1,0:T(8,128)}, u32[]{:S(2)}) copy-start(f32[5,16,16,128]{3,2,1,0:T(8,128)} %source.1) | copy-start | bytes 1966084
  4.9 6.2 %collective-permute-start = (f32[13,16,128]{2,1,0:T(8,128)S(1)}, f32[13,16,128]{2,1,0:T(8,128)S(1)}, u32[]{:S(2)}, u32[]{:S(2)}) collective-permute-start(f32[13,16,128]{2,1,0:T(8,128)S(1)} %get-tuple-element.11.y_own_near), channel_id=1, source_target_pairs={{0,1},{1,0},{2,3},{3,2},{4,5},{5,4},{6,7},{7,6},{8,9},{9,8},{10,11... | collective-permute-start | bytes 319496 | tf_op jit(solution)/shard_map/ppermute | solution.py:373
  8.9 2.1 %collective-permute-start.1 = (f32[13,16,128]{2,1,0:T(8,128)S(1)}, f32[13,16,128]{2,1,0:T(8,128)S(1)}, u32[]{:S(2)}, u32[]{:S(2)}) collective-permute-start(f32[13,16,128]{2,1,0:T(8,128)S(1)} %get-tuple-element.12.y_own_far), channel_id=1, source_target_pairs={{1,2},{2,1},{5,6},{6,5},{9,10},{10,9},{13,14},{14,13},{17,18},{18,... | collective-permute-start | bytes 319496 | tf_op jit(solution)/shard_map/ppermute | solution.py:372
  11.8 11.1 %collective-permute-start.3 = (f32[13,16,128]{2,1,0:T(8,128)S(1)}, f32[13,16,128]{2,1,0:T(8,128)S(1)}, u32[]{:S(2)}, u32[]{:S(2)}) collective-permute-start(f32[13,16,128]{2,1,0:T(8,128)S(1)} %edge_rows.3.x_own_far), channel_id=1, source_target_pairs={{4,8},{8,4},{12,16},{16,12},{20,24},{24,20},{28,32},{32,28},{36,40... | collective-permute-start | bytes 319496 | tf_op jit(solution)/shard_map/ppermute | solution.py:372
  17.3 5.3 %copy-start.5 = (f32[512]{0:T(512)S(1)}, f32[512]{0:T(512)}, u32[]{:S(2)}) copy-start(f32[512]{0:T(512)} %pressure_ref.1) | copy-start | bytes 6148
  17.3 5.3 %copy-start.6 = (s32[512,1]{0,1:T(1,128)S(1)}, s32[512,1]{0,1:T(1,128)}, u32[]{:S(2)}) copy-start(s32[512,1]{0,1:T(1,128)} %param.22) | copy-start | bytes 6148
  17.3 5.3 %copy-start.7 = (s32[512]{0:T(512)S(1)}, s32[512]{0:T(512)}, u32[]{:S(2)}) copy-start(s32[512]{0:T(512)} %local_ref.1) | copy-start | bytes 6148
  17.3 6.2 %copy-start.1 = (bf16[3,16,16,128]{3,2,1,0:T(8,128)(2,1)S(1)}, bf16[3,16,16,128]{3,2,1,0:T(8,128)(2,1)}, u32[]{:S(2)}) copy-start(bf16[3,16,16,128]{3,2,1,0:T(8,128)(2,1)} %velocity.1) | copy-start | bytes 589828
  18.1 4.6 %copy-start.4 = (s32[512]{0:T(512)S(1)}, s32[512]{0:T(512)}, u32[]{:S(2)}) copy-start(s32[512]{0:T(512)} %cell_ref.1) | copy-start | bytes 6148
  18.1 5.5 %collective-permute-start.2 = (f32[13,16,128]{2,1,0:T(8,128)S(1)}, f32[13,16,128]{2,1,0:T(8,128)S(1)}, u32[]{:S(2)}, u32[]{:S(2)}) collective-permute-start(f32[13,16,128]{2,1,0:T(8,128)S(1)} %edge_rows.2.after.x_own_near), channel_id=1, source_target_pairs={{0,4},{4,0},{8,12},{12,8},{16,20},{20,16},{24,28},{28,24},{32,36},... | collective-permute-start | bytes 319496 | tf_op jit(solution)/shard_map/ppermute | solution.py:373
  22.7 0.9 %copy-start.2 = (bf16[16,16,128]{2,1,0:T(8,128)(2,1)S(1)}, bf16[16,16,128]{2,1,0:T(8,128)(2,1)}, u32[]{:S(2)}) copy-start(bf16[16,16,128]{2,1,0:T(8,128)(2,1)} %dissip.1) | copy-start | bytes 196612

commit v3 on v2

--- a/solution.py
+++ b/solution.py
@@ -53,6 +53,16 @@
     return jnp.where(position % per_brick < limit, area, 0.0)
 
 
+class Splat:
+    def __init__(self, ref):
+        self.ref = ref
+
+    def __getitem__(self, at):
+        k, direction, c = at
+        i = (k * 3 + direction) * 5 + c
+        return self.ref[i:i + 1, :]
+
+
 def turn(jac, direction, values):
     out = []
     for c in range(5):
@@ -71,7 +81,7 @@
     return [scaled * turned[c] + spread * values[c] for c in range(5)]
 
 
-def relax_row(jac, here, x_low, x_high, edge_low, edge_high, source, speed, damping, wall):
+def relax_row(jac, here, lead_low, lead_high, edge_low, edge_high, source, speed, damping, wall, lead=0):
     rows, lanes = here[0].shape
     at_y = lax.broadcasted_iota(jnp.int32, (rows, lanes), 0)
     at_z = lax.broadcasted_iota(jnp.int32, (rows, lanes), 1)
@@ -80,9 +90,9 @@
     for direction in range(3):
         jumps = []
         for c in range(5):
-            if direction == 0:
-                low, high = x_low[c], x_high[c]
-            elif direction == 1:
+            if direction == lead:
+                low, high = lead_low[c], lead_high[c]
+            elif direction < 2:
                 low = jnp.where(at_y == 0, edge_low[c], pltpu.roll(here[c], 1, 0))
                 high = jnp.where(at_y == rows - 1, edge_high[c], pltpu.roll(here[c], rows - 1, 0))
             else:
@@ -122,20 +132,16 @@
         copy.wait()
 
 
-def first_kernel(per_brick, jac, counts, cell_hbm, angle_hbm, area_hbm, adjoint_hbm, source_hbm, velocity_hbm, dissip_hbm,
-                 partial, walls, near_out, far_out, near_end, far_end, face_out,
-                 cell_ref, angle_ref, area_ref, field, source, velocity, dissip, edges, sems):
+def first_kernel(per_brick, jac_hbm, counts_hbm, cell_hbm, angle_hbm, area_hbm, adjoint_hbm, source_hbm, velocity_hbm, dissip_hbm,
+                 walls, near_out, far_out, face_out, jac_out, jac, counts, cell_ref, angle_ref, area_ref, field, source, velocity, dissip,
+                 coefficient, sems):
     size_x, size_y, size_z = dissip.shape
     copies = start_all([(cell_hbm, cell_ref), (angle_hbm, angle_ref), (area_hbm, area_ref),
-                        (adjoint_hbm, field.at[:, pl.ds(1, size_x)]), (velocity_hbm, velocity),
-                        (dissip_hbm, dissip), (source_hbm, source)], sems)
-    side = 1 - lax.axis_index("blk") % 2
+                        (adjoint_hbm, field), (velocity_hbm, velocity),
+                        (dissip_hbm, dissip), (source_hbm, source), (counts_hbm, counts), (jac_hbm, jac)], sems)
+    odd = lax.axis_index("blk") % 2 == 1
     faces = cell_ref.shape[0]
-    blank = jnp.zeros((size_y, size_z), jnp.float32)
-    for c in range(5):
-        field[c, 0] = blank
-        field[c, size_x + 1] = blank
-    wait_all(copies[:3])
+    wait_all(copies[:3] + copies[7:8])
     cell = cell_ref[...].reshape(1, faces)
     area = area_ref[...].reshape(1, faces)
     normal = face_normals(angle_ref[...])
@@ -155,12 +161,40 @@
         total = dot_last(rows, jnp.concatenate(put, axis=0))
         walls[m] = total[:, :size_z].reshape(size_x, size_y, size_z)
         walls[m + 1] = total[:, size_z:].reshape(size_x, size_y, size_z)
-    wait_all(copies[3:])
+    wait_all(copies[3:7] + copies[8:])
+    for i in range(75):
+        jac_out[i:i + 1, :] = jnp.full((1, size_z), jac[i // 15, i // 5 % 3, i % 5], jnp.float32)
+
+    for d in range(3):
+        coefficient[d] = velocity[d].astype(jnp.float32)
+    coefficient[3] = dissip[...].astype(jnp.float32)
+    blank = jnp.zeros((size_x, size_z), jnp.float32)
+    column = lambda ref, count, y: [ref[c, :, y, :] for c in range(count)]
+    strips = []
+    for y in (0, size_y - 1):
+        here = column(field, 5, y)
+        inner = column(field, 5, 1 if y == 0 else size_y - 2)
+        below, above = ([blank] * 5, inner) if y == 0 else (inner, [blank] * 5)
+        *speed, damping = column(coefficient, 4, y)
+        sym = column(walls, 6, y)
+        wall = [[sym[SYM[a][b]] for b in range(3)] for a in range(3)]
+        zeros = [0.0] * 5
+        out = relax_row(jac, here, below, above, zeros, zeros, column(source, 5, y), speed, damping, wall, lead=1)
+        strips.append(here + out + [speed[1], damping, speed[0]])
+    for f, (low, high) in enumerate(zip(*strips)):
+        near_out[f] = jnp.where(odd, low, high)
+        far_out[f] = jnp.where(odd, high, low)
+
+
+def inner_kernel(jac_ref, adjoint, source, velocity, dissip, walls, partial, near_end, far_end):
+    size_x, size_y, size_z = dissip.shape
+    jac = Splat(jac_ref)
 
     def step(x, carry):
-        here = [field[c, x + 1] for c in range(5)]
-        below = [field[c, x] for c in range(5)]
-        above = [field[c, x + 2] for c in range(5)]
+        here = [adjoint[c, x] for c in range(5)]
+        has_low, has_high = jnp.where(x > 0, 1.0, 0.0), jnp.where(x < size_x - 1, 1.0, 0.0)
+        below = [adjoint[c, jnp.maximum(x - 1, 0)] * has_low for c in range(5)]
+        above = [adjoint[c, jnp.minimum(x + 1, size_x - 1)] * has_high for c in range(5)]
         zeros = [0.0] * 5
         src = [source[c, x] for c in range(5)]
         speed = [velocity[d, x].astype(jnp.float32) for d in range(3)]
@@ -170,27 +204,22 @@
         out = relax_row(jac, here, below, above, zeros, zeros, src, speed, damping, wall)
         for c in range(5):
             partial[c, x] = out[c]
-        fields = here + out + [speed[1], damping, speed[0]]
-        for f, edge in enumerate(fields):
-            edges[side, f, pl.ds(x, 1), :] = edge[0:1]
-            edges[1 - side, f, pl.ds(x, 1), :] = edge[size_y - 1:size_y]
         return carry
 
     lax.fori_loop(0, size_x, step, 0, unroll=2)
-    near_out[...] = edges[0]
-    far_out[...] = edges[1]
     odd = lax.axis_index("core")
     for out, x in ((near_end, (1 - odd) * (size_x - 1)), (far_end, odd * (size_x - 1))):
         for c in range(5):
-            out[c] = field[c, x + 1]
+            out[c] = adjoint[c, x]
             out[5 + c] = partial[c, x]
         out[10] = velocity[0, x].astype(jnp.float32)
         out[11] = dissip[x].astype(jnp.float32)
         out[12] = velocity[1, x].astype(jnp.float32)
 
 
-def edge_kernel(is_near, jac, from_near, from_far, mine, out):
+def edge_kernel(is_near, jac_ref, from_near, from_far, mine, out):
     rows, lanes = mine.shape[1:]
+    jac = Splat(jac_ref)
     at_y = lax.broadcasted_iota(jnp.int32, (rows, lanes), 0)
     odd_y = lax.axis_index("blk") % 2 == 1
     last = (lax.axis_index("core") == 1) != is_near
@@ -240,9 +269,10 @@
     plan[...] = jnp.concatenate(rows + [jnp.zeros((16 - len(rows), faces), jnp.float32)], axis=0)
 
 
-def third_kernel(parts, jac, plan, partial, walls, source, velocity, dissip, y_own_near, y_own_far, y_near, y_far,
+def third_kernel(parts, jac_ref, plan, partial, walls, source, velocity, dissip, y_own_near, y_own_far, y_near, y_far,
                  x_own_near, x_own_far, x_near, x_far, relaxed_hbm, message,
                  field, edge_low, edge_high, relaxed, out_sem):
+    jac = Splat(jac_ref)
     faces = plan.shape[1]
     size_x, size_y, size_z = dissip.shape
     for c in range(5):
@@ -384,7 +414,6 @@
     faces = cut_cell.shape[0]
     per_brick = faces // cut_counts.shape[0]
     f32 = jnp.float32
-    smem = pl.BlockSpec(memory_space=pltpu.SMEM)
     vmem = pl.BlockSpec(memory_space=pltpu.VMEM)
     hbm = pl.BlockSpec(memory_space=pltpu.HBM)
     shape = jax.ShapeDtypeStruct
@@ -400,27 +429,36 @@
     edge = shape((5, size_x, size_z), f32)
     far_memory = lambda *arrays: [pltpu.with_memory_space_constraint(a, pltpu.HBM) for a in arrays]
     far_memory = lambda *arrays: [pltpu.with_memory_space_constraint(a, pltpu.HBM) for a in arrays]
-    partial, walls, y_near_out, y_far_out, near_end, far_end, face = pl.pallas_call(
+    walls, y_near_out, y_far_out, face, jac_rows = pl.pallas_call(
         functools.partial(first_kernel, per_brick),
-        in_specs=[smem, smem] + [hbm] * 7,
-        out_specs=[vmem] * 7,
-        out_shape=[block, wall] + [strip] * 4 + [shape((8, faces), f32)],
-        scratch_shapes=scratch(cut_cell, face_angles, face_area, padded, source, velocity, dissip)
-        + [pltpu.VMEM((2,) + strip.shape, f32), dma((7,))],
+        in_specs=[hbm] * 9,
+        out_specs=[vmem] * 5,
+        out_shape=[wall, strip, strip, shape((8, faces), f32), shape((80, size_z), f32)],
+        scratch_shapes=[pltpu.SMEM(jacobian.shape, f32), pltpu.SMEM(cut_counts.shape, jnp.int32)] + scratch(cut_cell, face_angles, face_area, block, source, velocity, dissip)
+        + [pltpu.VMEM((4,) + dissip.shape, f32), dma((9,))],
+        compiler_params=ROOM,
+        name="first_columns",
+    )(*far_memory(jacobian, cut_counts, cut_cell, face_angles, face_area, adjoint, source, velocity, dissip))
+    from_near, from_far = swap("blk", y_near_out, y_far_out)
+
+    partial, near_end, far_end = pl.pallas_call(
+        inner_kernel,
+        in_specs=[vmem] * 6,
+        out_specs=[vmem] * 3,
+        out_shape=[block, strip, strip],
         compiler_params=ROOM,
         name="first_step",
-    )(*far_memory(jacobian, cut_counts, cut_cell, face_angles, face_area, adjoint, source, velocity, dissip))
-    from_near, from_far = swap("blk", y_near_out, y_far_out)
+    )(jac_rows, adjoint, source, velocity, dissip, walls)
 
     def edge_rows(is_near, end):
         return pl.pallas_call(
             functools.partial(edge_kernel, is_near),
-            in_specs=[smem] + [vmem] * 3,
+            in_specs=[vmem] * 4,
             out_specs=vmem,
             out_shape=strip,
             compiler_params=SMALL,
             name="edge_rows",
-        )(jacobian, from_near, from_far, end)
+        )(jac_rows, from_near, from_far, end)
 
     x_far_out = edge_rows(False, far_end)
     x_near_out = edge_rows(True, near_end)
@@ -437,13 +475,13 @@
 
     relaxed, message = pl.pallas_call(
         functools.partial(third_kernel, parts),
-        in_specs=[smem] + [vmem] * 14,
+        in_specs=[vmem] * 15,
         out_specs=[hbm, vmem],
         out_shape=[block, shape((n_y * n_c * n_x, 8 * n_z), f32)],
         scratch_shapes=scratch(padded, edge, edge, block) + [dma],
         compiler_params=ROOM,
         name="second_step",
-    )(jacobian, plan, partial, walls, source, velocity, dissip, y_near_out, y_far_out, from_near, from_far,
+    )(jac_rows, plan, partial, walls, source, velocity, dissip, y_near_out, y_far_out, from_near, from_far,
       x_near_out, x_far_out, x_near, x_far)
 
     got = lax.all_to_all(message, ("y", "core", "blk"), split_axis=0, concat_axis=0, tiled=True)

time: 69.6 us -> 66.4 us (0.954)
  Pallas kernels: 10.8 us -> 8.55 us
  waiting for transfers between devices: 2.12 us -> 0.73 us
    pallas_call x4 -> x5, Pallas kernels: 9.61 us -> 7.37 us  [the longest x1 3.21 us: on_device(): pl.pallas_call(functools.partial(third_kernel, parts), in_specs=[vmem] *...]
    ppermute x2, waiting for transfers between devices: 2.12 us -> 0.73 us  [swap(): return (lax.ppermute(near, axis, inside), from_far)]
    all_to_all x1, blocking collectives: 20.1 us -> 20.8 us  [on_device(): got = lax.all_to_all(turned, 'z', split_axis=0, concat_axis=0, tiled=True)]
  transfers between devices with their start and end apart: 4 -> 4, of which waited for: 2 -> 1; matrix products, arithmetic and copies ran while one was open for 0% -> 0% of each run, Pallas kernels for 1% -> 3%
where the time goes in v3:
time: 66.4 us; the launch traced here: 66.1 us
  blocking collectives  41.4 us (62%)
  starting transfers between devices  14.5 us (22%)
  Pallas kernels  8.55 us (13%)
  between operations  0.86 us (1%)
  waiting for transfers between devices  0.73 us (1%)
    all_to_all x1, blocking collectives, on_device(): got = lax.all_to_all(turned, 'z', split_axis=0, concat_axis=0, tiled=True)  20.8 us
    all_to_all x1, blocking collectives, on_device(): lax.all_to_all(message, ('y', 'core', 'blk'), split_axis=0, concat_axis=0...  20.7 us
    ppermute x2, starting transfers between devices, swap(): return (lax.ppermute(near, axis, inside), from_far)  8.46 us
    ppermute x2, starting transfers between devices, swap(): from_far = lax.ppermute(far, axis, across)  6 us
    pallas_call x1, Pallas kernels, on_device(): pl.pallas_call(functools.partial(third_kernel, parts), in_specs=[vmem] *...  3.21 us
    pallas_call x1, Pallas kernels, on_device(): pl.pallas_call(functools.partial(first_kernel, per_brick), in_specs=[hbm]...  2.57 us
    pallas_call x1, Pallas kernels, on_device(): pl.pallas_call(inner_kernel, in_specs=[vmem] * 6, out_specs=[vmem] * 3, o...  1.5 us
  transfers between devices with their start and end apart: 4, of which 1 were waited for; matrix products, arithmetic and copies ran while one was open for 0% of the time, Pallas kernels for 3%

profile of v3, /device:TPU:1, one launch (start us, length us, event | category | flops | bytes accessed | tf_op | source)
XLA Modules:
  0.0 66.1 jit_solution(16191864023989532042)
XLA Ops:
  0.6 0.0 copy-start
  0.6 0.0 copy-start.1
  0.7 0.0 copy-start.2
  0.7 0.0 copy-start.3
  0.7 2.6 %first_columns.1 = (f32[6,16,16,128]{3,2,1,0:T(8,128)S(1)}, f32[13,16,128]{2,1,0:T(8,128)S(1)}, f32[13,16,128]{2,1,0:T(8,128)S(1)}, f32[8,512]{1,0:T(8,128)S(1)}, f32[80,128]{1,0:T(8,128)S(1)}) custom-call(f32[5,3,5]{2,1,0:T(4,128)} %bitcast.13, s32[8]{0:T(128)} %counts_hbm.1, s32[512]{0:T(512)} %cell_ref.1, f32[2,512]{1,0:T(2,128)} %angle_hbm.1, ...), custom_call_target="tpu_custom_call" | custom-call | tf_op jit(solution)/shard_map/first_columns/pallas_call | solution.py:432
  3.2 3.9 %collective-permute-start = (f32[13,16,128]{2,1,0:T(8,128)S(1)}, f32[13,16,128]{2,1,0:T(8,128)S(1)}, u32[]{:S(2)}, u32[]{:S(2)}) collective-permute-start(f32[13,16,128]{2,1,0:T(8,128)S(1)} %get-tuple-element.13.y_own_near), channel_id=1, source_target_pairs={{0,1},{1,0},{2,3},{3,2},{4,5},{5,4},{6,7},{7,6},{8,9},{9,8},{10,11... | collective-permute-start | bytes 319496 | tf_op jit(solution)/shard_map/ppermute | solution.py:403
  7.2 0.7 %collective-permute-start.1 = (f32[13,16,128]{2,1,0:T(8,128)S(1)}, f32[13,16,128]{2,1,0:T(8,128)S(1)}, u32[]{:S(2)}, u32[]{:S(2)}) collective-permute-start(f32[13,16,128]{2,1,0:T(8,128)S(1)} %get-tuple-element.14.y_own_far), channel_id=1, source_target_pairs={{1,2},{2,1},{5,6},{6,5},{9,10},{10,9},{13,14},{14,13},{17,18},{18,... | collective-permute-start | bytes 319496 | tf_op jit(solution)/shard_map/ppermute | solution.py:402
  7.9 1.5 %first_step.1 = (f32[5,16,16,128]{3,2,1,0:T(8,128)S(1)}, f32[13,16,128]{2,1,0:T(8,128)S(1)}, f32[13,16,128]{2,1,0:T(8,128)S(1)}) custom-call(f32[80,128]{1,0:T(8,128)S(1)} %get-tuple-element.12.jac_ref, f32[5,16,16,128]{3,2,1,0:T(8,128)S(1)} %copy-done.1, f32[5,16,16,128]{3,2,1,0:T(8,128)S(1)} %copy-done, bf16[3,16,16,128]{3,2,1,0:T(8,128)(2,1)S(1)} %copy-done.2, ...), custom_call_target="tpu_custom_call" | custom-call | tf_op jit(solution)/shard_map/first_step/pallas_call | solution.py:444
  9.4 0.0 collective-permute-done.from_near.y_near
  9.4 0.0 collective-permute-done.1.from_far.y_far
  9.5 5.3 %collective-permute-start.3 = (f32[13,16,128]{2,1,0:T(8,128)S(1)}, f32[13,16,128]{2,1,0:T(8,128)S(1)}, u32[]{:S(2)}, u32[]{:S(2)}) collective-permute-start(f32[13,16,128]{2,1,0:T(8,128)S(1)} %edge_rows.3.x_own_far), channel_id=1, source_target_pairs={{4,8},{8,4},{12,16},{16,12},{20,24},{24,20},{28,32},{32,28},{36,40... | collective-permute-start | bytes 319496 | tf_op jit(solution)/shard_map/ppermute | solution.py:402
  14.8 0.0 copy-start.5
  14.9 0.0 copy-start.6
  14.9 0.0 copy-start.7
  14.9 0.0 copy-start.4
  15.0 4.5 %collective-permute-start.2 = (f32[13,16,128]{2,1,0:T(8,128)S(1)}, f32[13,16,128]{2,1,0:T(8,128)S(1)}, u32[]{:S(2)}, u32[]{:S(2)}) collective-permute-start(f32[13,16,128]{2,1,0:T(8,128)S(1)} %edge_rows.2.after.x_own_near), channel_id=1, source_target_pairs={{0,4},{4,0},{8,12},{12,8},{16,20},{20,16},{24,28},{28,24},{32,36},... | collective-permute-start | bytes 319496 | tf_op jit(solution)/shard_map/ppermute | solution.py:403
  19.5 0.2 face_plan.1.plan
  19.7 0.0 collective-permute-done.3.x_far
  19.7 0.7 %collective-permute-done.2.x_near = f32[13,16,128]{2,1,0:T(8,128)S(1)} collective-permute-done((f32[13,16,128]{2,1,0:T(8,128)S(1)}, f32[13,16,128]{2,1,0:T(8,128)S(1)}, u32[]{:S(2)}, u32[]{:S(2)}) %collective-permute-start.2) | collective-permute-done | bytes 106528 | tf_op jit(solution)/shard_map/ppermute | solution.py:403
  20.4 3.2 %second_step.1 = (f32[5,16,16,128]{3,2,1,0:T(8,128)}, f32[32,128]{1,0:T(8,128)S(1)}) custom-call(f32[80,128]{1,0:T(8,128)S(1)} %get-tuple-element.12.jac_ref, f32[16,512]{1,0:T(8,128)S(1)} %face_plan.1.plan, f32[5,16,16,128]{3,2,1,0:T(8,128)S(1)} %get-tuple-element.18.partial, f32[6,16,16,128]{3,2,1,0:T(8,128)S(1)} %get-tuple-element.15.walls, ...), custom_call_target="tpu_custom_call" | custom-call | tf_op jit(solution)/shard_map/second_step/pallas_call | solution.py:476
  23.6 20.7 %all_to_all.22 = f32[32,1,128]{2,1,0:T(1,128)S(1)} all-to-all(f32[32,1,128]{2,1,0:T(1,128)S(1)} %bitcast.11), channel_id=1, replica_groups=mesh['y'=4,'z'=16,'core'=2,'blk'=4] {'y','core','blk'}, dimensions={0} | all-to-all | bytes 32768 | tf_op jit(solution)/shard_map/all_to_all | solution.py:487
  44.3 0.1 turn_words.1
  44.4 20.8 %all_to_all.23 = f32[16,8,128]{2,1,0:T(8,128)S(1)} all-to-all(f32[16,8,128]{2,1,0:T(8,128)S(1)} %bitcast.8), channel_id=1, replica_groups=mesh['y'=4,'z'=16,'core'=2,'blk'=4] {'z'}, dimensions={0} | all-to-all | bytes 131072 | tf_op jit(solution)/shard_map/all_to_all | solution.py:496
  65.2 0.9 %sum_terms.1 = f32[3,256]{1,0:T(4,128)} custom-call(f32[128,128]{1,0:T(8,128)S(1)} %bitcast.9), custom_call_target="tpu_custom_call" | custom-call | tf_op jit(solution)/shard_map/sum_terms/pallas_call | solution.py:497
  (10 shorter events, 0.1 us)
Async XLA Ops:
  0.6 7.3 %copy-start = (f32[5,16,16,128]{3,2,1,0:T(8,128)S(1)}, f32[5,16,16,128]{3,2,1,0:T(8,128)}, u32[]{:S(2)}) copy-start(f32[5,16,16,128]{3,2,1,0:T(8,128)} %source.3) | copy-start | bytes 1966084
  0.6 7.3 %copy-start.1 = (f32[5,16,16,128]{3,2,1,0:T(8,128)S(1)}, f32[5,16,16,128]{3,2,1,0:T(8,128)}, u32[]{:S(2)}) copy-start(f32[5,16,16,128]{3,2,1,0:T(8,128)} %adjoint.1) | copy-start | bytes 1966084
  0.7 7.3 %copy-start.2 = (bf16[3,16,16,128]{3,2,1,0:T(8,128)(2,1)S(1)}, bf16[3,16,16,128]{3,2,1,0:T(8,128)(2,1)}, u32[]{:S(2)}) copy-start(bf16[3,16,16,128]{3,2,1,0:T(8,128)(2,1)} %velocity.3) | copy-start | bytes 589828
  0.7 7.3 %copy-start.3 = (bf16[16,16,128]{2,1,0:T(8,128)(2,1)S(1)}, bf16[16,16,128]{2,1,0:T(8,128)(2,1)}, u32[]{:S(2)}) copy-start(bf16[16,16,128]{2,1,0:T(8,128)(2,1)} %dissip.3) | copy-start | bytes 196612
  3.2 6.2 %collective-permute-start = (f32[13,16,128]{2,1,0:T(8,128)S(1)}, f32[13,16,128]{2,1,0:T(8,128)S(1)}, u32[]{:S(2)}, u32[]{:S(2)}) collective-permute-start(f32[13,16,128]{2,1,0:T(8,128)S(1)} %get-tuple-element.13.y_own_near), channel_id=1, source_target_pairs={{0,1},{1,0},{2,3},{3,2},{4,5},{5,4},{6,7},{7,6},{8,9},{9,8},{10,11... | collective-permute-start | bytes 319496 | tf_op jit(solution)/shard_map/ppermute | solution.py:403
  7.2 2.2 %collective-permute-start.1 = (f32[13,16,128]{2,1,0:T(8,128)S(1)}, f32[13,16,128]{2,1,0:T(8,128)S(1)}, u32[]{:S(2)}, u32[]{:S(2)}) collective-permute-start(f32[13,16,128]{2,1,0:T(8,128)S(1)} %get-tuple-element.14.y_own_far), channel_id=1, source_target_pairs={{1,2},{2,1},{5,6},{6,5},{9,10},{10,9},{13,14},{14,13},{17,18},{18,... | collective-permute-start | bytes 319496 | tf_op jit(solution)/shard_map/ppermute | solution.py:402
  9.5 10.2 %collective-permute-start.3 = (f32[13,16,128]{2,1,0:T(8,128)S(1)}, f32[13,16,128]{2,1,0:T(8,128)S(1)}, u32[]{:S(2)}, u32[]{:S(2)}) collective-permute-start(f32[13,16,128]{2,1,0:T(8,128)S(1)} %edge_rows.3.x_own_far), channel_id=1, source_target_pairs={{4,8},{8,4},{12,16},{16,12},{20,24},{24,20},{28,32},{32,28},{36,40... | collective-permute-start | bytes 319496 | tf_op jit(solution)/shard_map/ppermute | solution.py:402
  14.8 4.6 %copy-start.5 = (f32[512]{0:T(512)S(1)}, f32[512]{0:T(512)}, u32[]{:S(2)}) copy-start(f32[512]{0:T(512)} %pressure_ref.1) | copy-start | bytes 6148
  14.9 4.6 %copy-start.6 = (s32[512,1]{0,1:T(1,128)S(1)}, s32[512,1]{0,1:T(1,128)}, u32[]{:S(2)}) copy-start(s32[512,1]{0,1:T(1,128)} %param.22) | copy-start | bytes 6148
  14.9 4.6 %copy-start.7 = (s32[512]{0:T(512)S(1)}, s32[512]{0:T(512)}, u32[]{:S(2)}) copy-start(s32[512]{0:T(512)} %local_ref.1) | copy-start | bytes 6148
  14.9 4.6 %copy-start.4 = (s32[512]{0:T(512)S(1)}, s32[512]{0:T(512)}, u32[]{:S(2)}) copy-start(s32[512]{0:T(512)} %cell_ref.1) | copy-start | bytes 6148
  15.0 5.5 %collective-permute-start.2 = (f32[13,16,128]{2,1,0:T(8,128)S(1)}, f32[13,16,128]{2,1,0:T(8,128)S(1)}, u32[]{:S(2)}, u32[]{:S(2)}) collective-permute-start(f32[13,16,128]{2,1,0:T(8,128)S(1)} %edge_rows.2.after.x_own_near), channel_id=1, source_target_pairs={{0,4},{4,0},{8,12},{12,8},{16,20},{20,16},{24,28},{28,24},{32,36},... | collective-permute-start | bytes 319496 | tf_op jit(solution)/shard_map/ppermute | solution.py:403

commit v4 on v3

--- a/solution.py
+++ b/solution.py
@@ -340,9 +340,12 @@
             relaxed[c, x] = out[c]
         return carry
 
-    lax.fori_loop(0, size_x, step, 0, unroll=2)
-    done = pltpu.make_async_copy(relaxed, relaxed_hbm, out_sem)
-    done.start()
+    half = size_x // 2
+    parts_out = [pl.ds(h * half, half) for h in range(2)]
+    dones = [pltpu.make_async_copy(relaxed.at[:, at], relaxed_hbm.at[:, at], out_sem.at[h]) for h, at in enumerate(parts_out)]
+    for h in range(2):
+        lax.fori_loop(h * half, (h + 1) * half, step, 0, unroll=4)
+        dones[h].start()
 
     normal = [plan[c:c + 1] for c in range(3)]
     strength, rank, label = plan[3:4], plan[4:5], plan[5:6]
@@ -367,7 +370,7 @@
     target = one_hot(target_row, n_y * n_c * n_x)
     message[...] = dot_last(jnp.concatenate([target, target], axis=1),
                             jnp.concatenate([hot * high, hot * low], axis=1))
-    done.wait()
+    wait_all(dones)
 
 
 def turn_kernel(got, out):
@@ -478,7 +481,7 @@
         in_specs=[vmem] * 15,
         out_specs=[hbm, vmem],
         out_shape=[block, shape((n_y * n_c * n_x, 8 * n_z), f32)],
-        scratch_shapes=scratch(padded, edge, edge, block) + [dma],
+        scratch_shapes=scratch(padded, edge, edge, block) + [dma((2,))],
         compiler_params=ROOM,
         name="second_step",
     )(jac_rows, plan, partial, walls, source, velocity, dissip, y_near_out, y_far_out, from_near, from_far,

time: 66.4 us -> 65.8 us (level)
  no operation moved by 1% of the time
where the time goes in v4:
time: 65.8 us; the launch traced here: 65.5 us
  blocking collectives  41.4 us (63%)
  starting transfers between devices  14.5 us (22%)
  Pallas kernels  7.95 us (12%)
  between operations  0.86 us (1%)
  waiting for transfers between devices  0.73 us (1%)
    all_to_all x1, blocking collectives, on_device(): got = lax.all_to_all(turned, 'z', split_axis=0, concat_axis=0, tiled=True)  20.8 us
    all_to_all x1, blocking collectives, on_device(): lax.all_to_all(message, ('y', 'core', 'blk'), split_axis=0, concat_axis=0...  20.7 us
    ppermute x2, starting transfers between devices, swap(): return (lax.ppermute(near, axis, inside), from_far)  8.46 us
    ppermute x2, starting transfers between devices, swap(): from_far = lax.ppermute(far, axis, across)  6 us
    pallas_call x1, Pallas kernels, on_device(): pl.pallas_call(functools.partial(third_kernel, parts), in_specs=[vmem] *...  2.6 us
    pallas_call x1, Pallas kernels, on_device(): pl.pallas_call(functools.partial(first_kernel, per_brick), in_specs=[hbm]...  2.57 us
    pallas_call x1, Pallas kernels, on_device(): pl.pallas_call(inner_kernel, in_specs=[vmem] * 6, out_specs=[vmem] * 3, o...  1.5 us
  transfers between devices with their start and end apart: 4, of which 1 were waited for; matrix products, arithmetic and copies ran while one was open for 0% of the time, Pallas kernels for 3%

profile of v4, /device:TPU:1, one launch (start us, length us, event | category | flops | bytes accessed | tf_op | source)
XLA Modules:
  0.0 65.5 jit_solution(11345107319985305837)
XLA Ops:
  0.6 0.0 copy-start
  0.6 0.0 copy-start.1
  0.7 0.0 copy-start.2
  0.7 0.0 copy-start.3
  0.7 2.6 %first_columns.1 = (f32[6,16,16,128]{3,2,1,0:T(8,128)S(1)}, f32[13,16,128]{2,1,0:T(8,128)S(1)}, f32[13,16,128]{2,1,0:T(8,128)S(1)}, f32[8,512]{1,0:T(8,128)S(1)}, f32[80,128]{1,0:T(8,128)S(1)}) custom-call(f32[5,3,5]{2,1,0:T(4,128)} %bitcast.13, s32[8]{0:T(128)} %counts_hbm.1, s32[512]{0:T(512)} %cell_ref.1, f32[2,512]{1,0:T(2,128)} %angle_hbm.1, ...), custom_call_target="tpu_custom_call" | custom-call | tf_op jit(solution)/shard_map/first_columns/pallas_call | solution.py:435
  3.2 3.9 %collective-permute-start = (f32[13,16,128]{2,1,0:T(8,128)S(1)}, f32[13,16,128]{2,1,0:T(8,128)S(1)}, u32[]{:S(2)}, u32[]{:S(2)}) collective-permute-start(f32[13,16,128]{2,1,0:T(8,128)S(1)} %get-tuple-element.13.y_own_near), channel_id=1, source_target_pairs={{0,1},{1,0},{2,3},{3,2},{4,5},{5,4},{6,7},{7,6},{8,9},{9,8},{10,11... | collective-permute-start | bytes 319496 | tf_op jit(solution)/shard_map/ppermute | solution.py:406
  7.2 0.7 %collective-permute-start.1 = (f32[13,16,128]{2,1,0:T(8,128)S(1)}, f32[13,16,128]{2,1,0:T(8,128)S(1)}, u32[]{:S(2)}, u32[]{:S(2)}) collective-permute-start(f32[13,16,128]{2,1,0:T(8,128)S(1)} %get-tuple-element.14.y_own_far), channel_id=1, source_target_pairs={{1,2},{2,1},{5,6},{6,5},{9,10},{10,9},{13,14},{14,13},{17,18},{18,... | collective-permute-start | bytes 319496 | tf_op jit(solution)/shard_map/ppermute | solution.py:405
  7.9 1.5 %first_step.1 = (f32[5,16,16,128]{3,2,1,0:T(8,128)S(1)}, f32[13,16,128]{2,1,0:T(8,128)S(1)}, f32[13,16,128]{2,1,0:T(8,128)S(1)}) custom-call(f32[80,128]{1,0:T(8,128)S(1)} %get-tuple-element.12.jac_ref, f32[5,16,16,128]{3,2,1,0:T(8,128)S(1)} %copy-done.1, f32[5,16,16,128]{3,2,1,0:T(8,128)S(1)} %copy-done, bf16[3,16,16,128]{3,2,1,0:T(8,128)(2,1)S(1)} %copy-done.2, ...), custom_call_target="tpu_custom_call" | custom-call | tf_op jit(solution)/shard_map/first_step/pallas_call | solution.py:447
  9.4 0.0 collective-permute-done.from_near.y_near
  9.4 0.0 collective-permute-done.1.from_far.y_far
  9.5 5.3 %collective-permute-start.3 = (f32[13,16,128]{2,1,0:T(8,128)S(1)}, f32[13,16,128]{2,1,0:T(8,128)S(1)}, u32[]{:S(2)}, u32[]{:S(2)}) collective-permute-start(f32[13,16,128]{2,1,0:T(8,128)S(1)} %edge_rows.3.x_own_far), channel_id=1, source_target_pairs={{4,8},{8,4},{12,16},{16,12},{20,24},{24,20},{28,32},{32,28},{36,40... | collective-permute-start | bytes 319496 | tf_op jit(solution)/shard_map/ppermute | solution.py:405
  14.8 0.0 copy-start.5
  14.9 0.0 copy-start.6
  14.9 0.0 copy-start.7
  14.9 0.0 copy-start.4
  15.0 4.5 %collective-permute-start.2 = (f32[13,16,128]{2,1,0:T(8,128)S(1)}, f32[13,16,128]{2,1,0:T(8,128)S(1)}, u32[]{:S(2)}, u32[]{:S(2)}) collective-permute-start(f32[13,16,128]{2,1,0:T(8,128)S(1)} %edge_rows.2.after.x_own_near), channel_id=1, source_target_pairs={{0,4},{4,0},{8,12},{12,8},{16,20},{20,16},{24,28},{28,24},{32,36},... | collective-permute-start | bytes 319496 | tf_op jit(solution)/shard_map/ppermute | solution.py:406
  19.5 0.2 face_plan.1.plan
  19.7 0.0 collective-permute-done.3.x_far
  19.7 0.7 %collective-permute-done.2.x_near = f32[13,16,128]{2,1,0:T(8,128)S(1)} collective-permute-done((f32[13,16,128]{2,1,0:T(8,128)S(1)}, f32[13,16,128]{2,1,0:T(8,128)S(1)}, u32[]{:S(2)}, u32[]{:S(2)}) %collective-permute-start.2) | collective-permute-done | bytes 106528 | tf_op jit(solution)/shard_map/ppermute | solution.py:406
  20.4 2.6 %second_step.1 = (f32[5,16,16,128]{3,2,1,0:T(8,128)}, f32[32,128]{1,0:T(8,128)S(1)}) custom-call(f32[80,128]{1,0:T(8,128)S(1)} %get-tuple-element.12.jac_ref, f32[16,512]{1,0:T(8,128)S(1)} %face_plan.1.plan, f32[5,16,16,128]{3,2,1,0:T(8,128)S(1)} %get-tuple-element.18.partial, f32[6,16,16,128]{3,2,1,0:T(8,128)S(1)} %get-tuple-element.15.walls, ...), custom_call_target="tpu_custom_call" | custom-call | tf_op jit(solution)/shard_map/second_step/pallas_call | solution.py:479
  23.0 20.7 %all_to_all.22 = f32[32,1,128]{2,1,0:T(1,128)S(1)} all-to-all(f32[32,1,128]{2,1,0:T(1,128)S(1)} %bitcast.11), channel_id=1, replica_groups=mesh['y'=4,'z'=16,'core'=2,'blk'=4] {'y','core','blk'}, dimensions={0} | all-to-all | bytes 32768 | tf_op jit(solution)/shard_map/all_to_all | solution.py:490
  43.7 0.1 turn_words.1
  43.8 20.8 %all_to_all.23 = f32[16,8,128]{2,1,0:T(8,128)S(1)} all-to-all(f32[16,8,128]{2,1,0:T(8,128)S(1)} %bitcast.8), channel_id=1, replica_groups=mesh['y'=4,'z'=16,'core'=2,'blk'=4] {'z'}, dimensions={0} | all-to-all | bytes 131072 | tf_op jit(solution)/shard_map/all_to_all | solution.py:499
  64.6 0.9 %sum_terms.1 = f32[3,256]{1,0:T(4,128)} custom-call(f32[128,128]{1,0:T(8,128)S(1)} %bitcast.9), custom_call_target="tpu_custom_call" | custom-call | tf_op jit(solution)/shard_map/sum_terms/pallas_call | solution.py:500
  (10 shorter events, 0.1 us)
Async XLA Ops:
  0.6 7.3 %copy-start = (f32[5,16,16,128]{3,2,1,0:T(8,128)S(1)}, f32[5,16,16,128]{3,2,1,0:T(8,128)}, u32[]{:S(2)}) copy-start(f32[5,16,16,128]{3,2,1,0:T(8,128)} %source.3) | copy-start | bytes 1966084
  0.6 7.3 %copy-start.1 = (f32[5,16,16,128]{3,2,1,0:T(8,128)S(1)}, f32[5,16,16,128]{3,2,1,0:T(8,128)}, u32[]{:S(2)}) copy-start(f32[5,16,16,128]{3,2,1,0:T(8,128)} %adjoint.1) | copy-start | bytes 1966084
  0.7 7.3 %copy-start.2 = (bf16[3,16,16,128]{3,2,1,0:T(8,128)(2,1)S(1)}, bf16[3,16,16,128]{3,2,1,0:T(8,128)(2,1)}, u32[]{:S(2)}) copy-start(bf16[3,16,16,128]{3,2,1,0:T(8,128)(2,1)} %velocity.3) | copy-start | bytes 589828
  0.7 7.3 %copy-start.3 = (bf16[16,16,128]{2,1,0:T(8,128)(2,1)S(1)}, bf16[16,16,128]{2,1,0:T(8,128)(2,1)}, u32[]{:S(2)}) copy-start(bf16[16,16,128]{2,1,0:T(8,128)(2,1)} %dissip.3) | copy-start | bytes 196612
  3.2 6.2 %collective-permute-start = (f32[13,16,128]{2,1,0:T(8,128)S(1)}, f32[13,16,128]{2,1,0:T(8,128)S(1)}, u32[]{:S(2)}, u32[]{:S(2)}) collective-permute-start(f32[13,16,128]{2,1,0:T(8,128)S(1)} %get-tuple-element.13.y_own_near), channel_id=1, source_target_pairs={{0,1},{1,0},{2,3},{3,2},{4,5},{5,4},{6,7},{7,6},{8,9},{9,8},{10,11... | collective-permute-start | bytes 319496 | tf_op jit(solution)/shard_map/ppermute | solution.py:406
  7.2 2.2 %collective-permute-start.1 = (f32[13,16,128]{2,1,0:T(8,128)S(1)}, f32[13,16,128]{2,1,0:T(8,128)S(1)}, u32[]{:S(2)}, u32[]{:S(2)}) collective-permute-start(f32[13,16,128]{2,1,0:T(8,128)S(1)} %get-tuple-element.14.y_own_far), channel_id=1, source_target_pairs={{1,2},{2,1},{5,6},{6,5},{9,10},{10,9},{13,14},{14,13},{17,18},{18,... | collective-permute-start | bytes 319496 | tf_op jit(solution)/shard_map/ppermute | solution.py:405
  9.5 10.2 %collective-permute-start.3 = (f32[13,16,128]{2,1,0:T(8,128)S(1)}, f32[13,16,128]{2,1,0:T(8,128)S(1)}, u32[]{:S(2)}, u32[]{:S(2)}) collective-permute-start(f32[13,16,128]{2,1,0:T(8,128)S(1)} %edge_rows.3.x_own_far), channel_id=1, source_target_pairs={{4,8},{8,4},{12,16},{16,12},{20,24},{24,20},{28,32},{32,28},{36,40... | collective-permute-start | bytes 319496 | tf_op jit(solution)/shard_map/ppermute | solution.py:405
  14.8 4.6 %copy-start.5 = (f32[512]{0:T(512)S(1)}, f32[512]{0:T(512)}, u32[]{:S(2)}) copy-start(f32[512]{0:T(512)} %pressure_ref.1) | copy-start | bytes 6148
  14.9 4.6 %copy-start.6 = (s32[512,1]{0,1:T(1,128)S(1)}, s32[512,1]{0,1:T(1,128)}, u32[]{:S(2)}) copy-start(s32[512,1]{0,1:T(1,128)} %param.22) | copy-start | bytes 6148
  14.9 4.6 %copy-start.7 = (s32[512]{0:T(512)S(1)}, s32[512]{0:T(512)}, u32[]{:S(2)}) copy-start(s32[512]{0:T(512)} %local_ref.1) | copy-start | bytes 6148
  14.9 4.6 %copy-start.4 = (s32[512]{0:T(512)S(1)}, s32[512]{0:T(512)}, u32[]{:S(2)}) copy-start(s32[512]{0:T(512)} %cell_ref.1) | copy-start | bytes 6148
  15.0 5.5 %collective-permute-start.2 = (f32[13,16,128]{2,1,0:T(8,128)S(1)}, f32[13,16,128]{2,1,0:T(8,128)S(1)}, u32[]{:S(2)}, u32[]{:S(2)}) collective-permute-start(f32[13,16,128]{2,1,0:T(8,128)S(1)} %edge_rows.2.after.x_own_near), channel_id=1, source_target_pairs={{0,4},{4,0},{8,12},{12,8},{16,20},{20,16},{24,28},{28,24},{32,36},... | collective-permute-start | bytes 319496 | tf_op jit(solution)/shard_map/ppermute | solution.py:406
